TPU v7x, 512 devices: a whole 4x8x8 slice. The times are simulated.
512 devices in a mesh: sec: 32 (over y, x), term: 16 (over z, core).
Axes of the slice: x: 4, y: 8, z: 8, core: 2. Of those that a mesh axis runs over, the one named last changes fastest.
Arguments:
- psi: bfloat16 [3, 512, 128, 128], P(None, 'sec'), may hold values from -6 to 6
- left_env: bfloat16 [64, 64, 128, 128], P('term', 'sec'), may hold values from -0.5 to 0.5
- right_env: bfloat16 [64, 64, 128, 128], P('term', 'sec'), may hold values from -0.0625 to 0.0625
- left_pick: int32 [512], P('sec'), may hold values from 0 to 1
- right_owner: int32 [512], replicated, may hold values from 0 to 31, as said below
- right_pick: int32 [512], replicated, may hold values from 0 to 1
Outputs:
- sigma: bfloat16 [3, 1024, 128, 128], P(None, 'sec', 'term')
Inputs may be any that keep to these rules, and one draw needn't show every extreme that they name: `right_owner`: within the 16 blocks of one device (aligned blocks of the index) each owner appears either 0 or 1 times; some owner appears 1 times in every device's blocks.
All inputs are finite; a program needn't handle non-finite values.
Results may differ from a plain program's by a relative error of at most 0.023.
Values may be sent and summed in bfloat16 or wider, within the bound.
No kernel may reach another device: no remote copies, remote signals or barrier semaphores. Data moves between devices by JAX's collectives and lax.ppermute only.
A program may use at most 128 MiB of HBM per device.

v0:
```python
import jax
import jax.numpy as jnp
from jax import lax
from jax.sharding import PartitionSpec as P

PAIR_DEV = 16


def slot_tables(right_owner, right_pick, slots, owner_here):
    rows = right_owner.reshape(-1, PAIR_DEV)
    picks = right_pick.reshape(-1, PAIR_DEV)
    same = rows[:, :, None] == rows[:, None, :]
    idx = jnp.arange(PAIR_DEV)
    earlier = idx[None, :] < idx[:, None]
    rank = jnp.sum((same & earlier[None]).astype(jnp.int32), axis=2)
    send_slot = rows * slots + rank
    slot_ids = jnp.arange(slots, dtype=jnp.int32)
    match = (rows == owner_here)[:, None, :] & (rank[:, None, :] == slot_ids[None, :, None])
    recv_pick = jnp.sum(jnp.where(match, picks[:, None, :], 0), axis=2).reshape(-1)
    recv_valid = jnp.any(match, axis=2).reshape(-1)
    return (send_slot, recv_pick, recv_valid)


def shards(psi, left_env, right_env, left_pick, right_owner, right_pick):
    groups = lax.axis_size("sec")
    slots = 2 * PAIR_DEV // groups
    recv_count = groups * slots
    here = lax.axis_index("sec")
    send_slot, recv_pick, recv_valid = slot_tables(right_owner, right_pick, slots, here)
    my_slot = jnp.take(send_slot, here, axis=0)
    left_sel = jnp.take(left_env, left_pick, axis=1)
    half = jnp.einsum("tjab,vjbc->jtvac", left_sel, psi, preferred_element_type=jnp.float32).astype(
        jnp.bfloat16
    )
    outgoing = jnp.zeros((recv_count,) + half.shape[1:], jnp.bfloat16).at[my_slot].set(half)
    arrived = lax.all_to_all(outgoing, "sec", split_axis=0, concat_axis=0, tiled=True)
    right_sel = jnp.take(right_env, recv_pick, axis=1)
    partial_sum = jnp.einsum(
        "stvab,tsbc->vsac", arrived, right_sel, preferred_element_type=jnp.float32
    )
    summed = lax.psum_scatter(
        partial_sum.astype(jnp.bfloat16), "term", scatter_dimension=2, tiled=True
    )
    return summed


def solution(mesh):
    return jax.shard_map(
        shards,
        mesh=mesh,
        in_specs=(
            P(None, "sec", None, None),
            P("term", "sec", None, None),
            P("term", "sec", None, None),
            P("sec"),
            P(),
            P(),
        ),
        out_specs=P(None, "sec", "term", None),
        check_vma=False,
    )
```

profile of v0, /device:TPU:2, one launch (start us, length us, event | category | flops | bytes accessed | tf_op | source)
XLA Modules:
  0.0 460.5 jit_solution(8016878103378933220)
XLA Ops:
  6.5 0.0 copy-start
  6.5 0.8 compare_select_fusion
  7.3 0.7 compare_and_fusion
  8.0 0.8 eq.53
  8.7 0.1 copy.28
  8.8 0.1 convert_reduce_fusion
  8.9 0.2 fusion.14
  9.1 3.1 gather_fusion.1
  12.3 0.0 copy-done
  12.3 6.0 %convert_bitcast_fusion = bf16[16,4,3,128,128]{4,3,2,1,0:T(8,128)(2,1)} fusion(bf16[16,4,128,128]{3,2,1,0:T(8,128)(2,1)} %gather_fusion.1, pred[16]{0:T(512)(128)(4,1)S(1)} %compare_and_fusion, bf16[3,16,128,128]{3,2,1,0:T(8,128)(2,1)S(1)} %copy-done), kind=kOutput, calls=%fused_computation.4 | convolution fusion | flops 809500672 | bytes 9961488 | tf_op jit(solution)/shard_map/tjab,vjbc->jtvac/dot_general | solution.py:32
  18.3 7.8 %broadcast_in_dim.43 = bf16[32,4,3,128,128]{4,3,2,1,0:T(8,128)(2,1)} broadcast(bf16[]{:T(256)} %constant.51.clone.1), dimensions={} | broadcast | bytes 12582914 | tf_op jit(solution)/shard_map/broadcast_in_dim | solution.py:35
  26.1 19.0 %scatter_fusion = bf16[32,4,3,128,128]{4,3,2,1,0:T(8,128)(2,1)} fusion(bf16[32,4,3,128,128]{4,3,2,1,0:T(8,128)(2,1)} %broadcast_in_dim.43, s32[16]{0:T(128)S(1)} %fusion.16, bf16[16,4,3,128,128]{4,3,2,1,0:T(8,128)(2,1)} %convert_bitcast_fusion), kind=kCustom, calls=%fused_computation.2 | custom fusion | bytes 18874432 | tf_op jit(solution)/shard_map/scatter | solution.py:35
  45.1 11.9 %copy.34 = bf16[32,4,3,128,128]{4,3,1,2,0:T(8,128)(2,1)} copy(bf16[32,4,3,128,128]{4,3,2,1,0:T(8,128)(2,1)} %scatter_fusion) | data formatting | bytes 25165824 | tf_op jit(solution)/shard_map/scatter | solution.py:35
  57.0 0.0 copy-start.2
  57.0 0.0 copy-start.3
  57.0 0.0 copy-start.1
  57.0 10.8 %all-to-all-start = ((bf16[32,4,3,128,128]{4,3,1,2,0:T(8,128)(2,1)}), bf16[32,4,3,128,128]{4,3,1,2,0:T(8,128)(2,1)}, u32[]{:S(2)}, u32[]{:S(2)}) async-start(bf16[32,4,3,128,128]{4,3,1,2,0:T(8,128)(2,1)} %copy.34), calls=%async_computation | async-start | bytes 25165824 | tf_op jit(solution)/shard_map/all_to_all | solution.py:36
  67.8 0.0 reduce-scatter.2.cloned.1.call-start
  67.8 0.0 copy-done.2
  67.8 0.1 eq.52
  67.9 0.1 copy.30
  68.0 0.0 copy-done.3
  68.0 0.1 broadcast_in_dim_reshape.2
  68.1 0.1 copy.31
  68.2 0.0 copy-done.1
  68.2 3.1 gather_fusion
  71.3 281.1 %all-to-all-done = bf16[32,4,3,128,128]{4,3,1,2,0:T(8,128)(2,1)} async-done(((bf16[32,4,3,128,128]{4,3,1,2,0:T(8,128)(2,1)}), bf16[32,4,3,128,128]{4,3,1,2,0:T(8,128)(2,1)}, u32[]{:S(2)}, u32[]{:S(2)}) %all-to-all-start) | async-done | bytes 12582944 | tf_op jit(solution)/shard_map/all_to_all | solution.py:36
  352.4 10.0 %fusion.4 = bf16[3,32,128,128]{2,3,0,1:T(8,128)(2,1)} fusion(bf16[32,4,3,128,128]{4,3,1,2,0:T(8,128)(2,1)} %all-to-all-done, bf16[32,4,128,128]{3,2,1,0:T(8,128)(2,1)} %gather_fusion, pred[32]{0:T(512)(128)(4,1)S(1)} %compare_and_fusion.1), kind=kOutput, calls=%fused_computation.9 | convolution fusion | flops 1614282752 | bytes 19922976 | tf_op jit(solution)/shard_map/stvab,tsbc->vsac/dot_general | solution.py:38
  362.4 4.9 %copy.36 = bf16[3,32,128,128]{3,1,0,2:T(8,128)(2,1)} copy(bf16[3,32,128,128]{2,3,0,1:T(8,128)(2,1)} %fusion.4) | data formatting | bytes 6291456 | tf_op jit(solution)/shard_map/convert_element_type | solution.py:42
  367.3 0.0 reduce-scatter.2.cloned.1.call-update
  367.3 84.7 %reduce-scatter.2.cloned.1.call-done = bf16[3,32,8,128]{3,1,0,2:T(8,128)(2,1)} async-done(((bf16[3,32,128,128]{3,1,0,2:T(8,128)(2,1)}), bf16[3,32,8,128]{3,1,0,2:T(8,128)(2,1)}) %reduce-scatter.2.cloned.1.call-update) | async-done | bytes 196624 | tf_op jit(solution)/shard_map/reduce_scatter | solution.py:41
  452.0 1.7 copy.37
  (8 shorter events, 0.1 us)
Async XLA Ops:
  6.5 5.7 %copy-start = (bf16[3,16,128,128]{3,2,1,0:T(8,128)(2,1)S(1)}, bf16[3,16,128,128]{3,2,1,0:T(8,128)(2,1)}, u32[]{:S(2)}) copy-start(bf16[3,16,128,128]{3,2,1,0:T(8,128)(2,1)} %param.6) | copy-start | bytes 4718596
  57.0 10.8 %copy-start.2 = (s32[512]{0:T(512)S(1)}, s32[512]{0:T(512)}, u32[]{:S(2)}) copy-start(s32[512]{0:T(512)} %param.10) | copy-start | bytes 6148
  57.0 11.0 %copy-start.3 = (s32[512]{0:T(512)S(1)}, s32[512]{0:T(512)}, u32[]{:S(2)}) copy-start(s32[512]{0:T(512)} %param.11) | copy-start | bytes 6148
  57.0 11.2 %copy-start.1 = (bf16[4,2,128,128]{3,2,1,0:T(8,128)(2,1)S(1)}, bf16[4,2,128,128]{3,2,1,0:T(8,128)(2,1)}, u32[]{:S(2)}) copy-start(bf16[4,2,128,128]{3,2,1,0:T(8,128)(2,1)} %param.8) | copy-start | bytes 786436
  57.0 295.4 %all-to-all-start = ((bf16[32,4,3,128,128]{4,3,1,2,0:T(8,128)(2,1)}), bf16[32,4,3,128,128]{4,3,1,2,0:T(8,128)(2,1)}, u32[]{:S(2)}, u32[]{:S(2)}) async-start(bf16[32,4,3,128,128]{4,3,1,2,0:T(8,128)(2,1)} %copy.34), calls=%async_computation | async-start | bytes 25165824 | tf_op jit(solution)/shard_map/all_to_all | solution.py:36
  67.8 384.2 %reduce-scatter.2.cloned.1.call-start = ((), (), s32[]{:S(2)}) async-start(), calls=%async_computation.2 | async-start | bytes 3342336 | tf_op jit(solution)/shard_map/reduce_scatter | solution.py:41
Sparse Core Ops, SparseCore 0:
  367.4 84.5 reduce-scatter.1
where the time goes:
time: 461 us
  waiting for transfers between devices  366 us (79%)
  local copies, waits for them, and re-layouts  52.6 us (11%)
  matrix products  16.1 us (3%)
  between operations  13.5 us (3%)
  starting transfers between devices  10.8 us (2%)
    all_to_all x1, waiting for transfers between devices, shards(): lax.all_to_all(outgoing, 'sec', split_axis=0, concat_axis=0, tiled=True)  281 us
    reduce_scatter x1, waiting for transfers between devices, shards(): lax.psum_scatter(partial_sum.astype(jnp.bfloat16), 'term', scatter_dimens...  84.7 us
    scatter x2, local copies, waits for them, and re-layouts, shards(): jnp.zeros((recv_count,) + half.shape[1:], jnp.bfloat16).at[my_slot]  30.9 us
    all_to_all x1, starting transfers between devices, shards(): lax.all_to_all(outgoing, 'sec', split_axis=0, concat_axis=0, tiled=True)  10.8 us
    dot_general x1, matrix products, shards(): jnp.einsum('stvab,tsbc->vsac', arrived, right_sel, preferred_element_type...  10 us
  transfers between devices with their start and end apart: 2, of which 2 were waited for; matrix products, arithmetic and copies ran while one was open for 1% of the time, Pallas kernels for 0%

commit v1 on v0

v1 whole, which is shorter than its diff:
```python
import jax
import jax.numpy as jnp
from jax import lax
from jax.experimental import pallas as pl
from jax.experimental.pallas import tpu as pltpu
from jax.sharding import PartitionSpec as P

B = 128
VECS = 3
PAIR_DEV = 16
TERM_DEV = 4
NX = 4
NY = 8
NZ = 8
HALF_Y = NY // 2
ENV_ROWS = TERM_DEV * 2 * B
PICK_ROWS = 16
ROWS = 8

X_GROUPS = [[y * NX + x for x in range(NX)] for y in range(NY)]
Y_GROUPS = [[y * NX + x for y in range(NY)] for x in range(NX)]
YZ_GROUPS = [
    [(y * NX + x) * 2 * NZ + z * 2 + c for y in range(NY) for z in range(NZ)]
    for x in range(NX)
    for c in range(2)
]
CORE_SWAP = [(z * 2 + c, z * 2 + 1 - c) for z in range(NZ) for c in range(2)]


def pack_kernel(where_ref, owner_ref, pick_ref, psi_ref, left_ref, psi_out, left_out, table, tile, sems):
    here, core = where_ref[0], where_ref[1]

    def clear(i, _):
        table[i] = 0
        return 0

    lax.fori_loop(0, NX * NY, clear, 0)

    def fill(j, _):
        table[owner_ref[here * PAIR_DEV + j]] = j
        return 0

    lax.fori_loop(0, PAIR_DEV, fill, 0)
    copies = []
    for x in range(NX):
        for i in range(HALF_Y):
            src = table[(core * HALF_Y + i) * NX + x]
            copies.append(
                pltpu.make_async_copy(psi_ref.at[:, src], psi_out.at[x, i], sems.at[x * HALF_Y + i])
            )
    for x in range(NX):
        copies.append(
            pltpu.make_async_copy(
                left_ref, left_out.at[x, pl.ds(0, ENV_ROWS)], sems.at[NX * HALF_Y + x]
            )
        )
    for copy in copies:
        copy.start()
    row = lax.broadcasted_iota(jnp.int32, (PICK_ROWS, B), 0)
    for x in range(NX):
        value = jnp.zeros((PICK_ROWS, B), jnp.int32)
        for y in range(NY):
            value = jnp.where(row == y, pick_ref[table[y * NX + x]], value)
        tile[x] = value.astype(jnp.float32).astype(jnp.bfloat16)
    last = pltpu.make_async_copy(
        tile, left_out.at[:, pl.ds(ENV_ROWS, PICK_ROWS)], sems.at[NX * HALF_Y + NX]
    )
    last.start()
    for copy in copies:
        copy.wait()
    last.wait()


def pack(where, right_owner, left_pick, psi, left):
    smem = pl.BlockSpec(memory_space=pltpu.SMEM)
    hbm = pl.BlockSpec(memory_space=pl.ANY)
    return pl.pallas_call(
        pack_kernel,
        out_shape=(
            jax.ShapeDtypeStruct((NX, HALF_Y, VECS, B, B), jnp.bfloat16),
            jax.ShapeDtypeStruct((NX, ENV_ROWS + PICK_ROWS, B), jnp.bfloat16),
        ),
        in_specs=[smem, smem, smem, hbm, hbm],
        out_specs=(hbm, hbm),
        scratch_shapes=[
            pltpu.SMEM((NX * NY,), jnp.int32),
            pltpu.VMEM((NX, PICK_ROWS, B), jnp.bfloat16),
            pltpu.SemaphoreType.DMA((NX * HALF_Y + NX + 1,)),
        ],
        name="pack",
    )(where, right_owner, left_pick, psi, left)


def half_kernel(where_ref, own_ref, other_ref, left_ref, half_ref):
    group, i = pl.program_id(0), pl.program_id(1)
    right_y = ((group + where_ref[1]) % 2) * HALF_Y + i

    def work(psi_ref):
        for x in range(NX):
            picks = left_ref[x, pl.ds(ENV_ROWS, PICK_ROWS), :].astype(jnp.float32)
            row = lax.broadcasted_iota(jnp.int32, (PICK_ROWS, B), 0)
            second = jnp.max(jnp.where(row == right_y, picks, 0.0), axis=0, keepdims=True) > 0.5
            second = jnp.broadcast_to(second, (B, B))
            lefts = []
            for t in range(TERM_DEV):
                first_env = left_ref[x, pl.ds((t * 2) * B, B), :]
                second_env = left_ref[x, pl.ds((t * 2 + 1) * B, B), :]
                lefts.append(jnp.where(second, second_env, first_env))
            lefts = jnp.concatenate(lefts, axis=0)
            vecs = jnp.concatenate([psi_ref[x, 0, v] for v in range(VECS)], axis=1)
            prod = jnp.dot(lefts, vecs, preferred_element_type=jnp.float32).astype(jnp.bfloat16)
            for t in range(TERM_DEV):
                for v in range(VECS):
                    half_ref[0, x, pl.ds(v * B, B), pl.ds(t * B, B)] = prod[
                        t * B : (t + 1) * B, v * B : (v + 1) * B
                    ]

    @pl.when(group == 0)
    def _():
        work(own_ref)

    @pl.when(group == 1)
    def _():
        work(other_ref)


def half_products(where, own, other, left):
    def psi_block(keep):
        return pl.BlockSpec(
            (NX, 1, VECS, B, B),
            lambda g, i, where_ref: (0, jnp.where(g == keep, i, (HALF_Y - 1) * (1 - keep)), 0, 0, 0),
        )

    return pl.pallas_call(
        half_kernel,
        out_shape=jax.ShapeDtypeStruct((NY, NX, VECS * B, TERM_DEV * B), jnp.bfloat16),
        grid_spec=pltpu.PrefetchScalarGridSpec(
            num_scalar_prefetch=1,
            grid=(2, HALF_Y),
            in_specs=[
                psi_block(0),
                psi_block(1),
                pl.BlockSpec((NX, ENV_ROWS + PICK_ROWS, B), lambda g, i, where_ref: (0, 0, 0)),
            ],
            out_specs=pl.BlockSpec(
                (1, NX, VECS * B, TERM_DEV * B),
                lambda g, i, where_ref: (((g + where_ref[1]) % 2) * HALF_Y + i, 0, 0, 0),
            ),
        ),
        compiler_params=pltpu.CompilerParams(vmem_limit_bytes=32 * 1024 * 1024),
        cost_estimate=pl.CostEstimate(
            flops=2 * NY * NX * VECS * TERM_DEV * B**3, bytes_accessed=17 * 2**20, transcendentals=0
        ),
        name="half",
    )(where, own, other, left)


def part_kernel(where_ref, owner_ref, pick_ref, half_ref, right_ref, keep_ref, give_ref, table):
    right_y = pl.program_id(0)
    here, core = where_ref[0], where_ref[1]
    my_y, my_x = here // NX, here % NX

    @pl.when(right_y == 0)
    def _():
        def clear(i, _):
            table[i] = 0
            return 0

        lax.fori_loop(0, NX * NY, clear, 0)

        def fill(j, _):
            block = my_y * NX * PAIR_DEV + j
            owner = owner_ref[block]
            slot = jnp.where(owner % NX == my_x, (j // PAIR_DEV) * NY + owner // NX, NX * NY)
            table[slot] = pick_ref[block]
            return 0

        lax.fori_loop(0, NX * PAIR_DEV, fill, 0)

    groups = [[[] for _ in range(NZ)] for _ in range(2)]
    for x in range(NX):
        pick = table[x * NY + right_y]
        rights = jnp.concatenate([right_ref[0, t * 2 + pick] for t in range(TERM_DEV)], axis=0)
        prod = jnp.dot(half_ref[0, x], rights, preferred_element_type=jnp.float32)
        for v in range(VECS):
            for z in range(NZ):
                for c in range(2):
                    at = v * B + (z * 2 + c) * ROWS
                    groups[c][z].append(prod[at : at + ROWS])
    packed = [
        [jnp.concatenate(groups[c][z], axis=0).astype(jnp.bfloat16) for z in range(NZ)] for c in range(2)
    ]

    @pl.when(core == 0)
    def _():
        for z in range(NZ):
            keep_ref[0, z] = packed[0][z]
            give_ref[0, z] = packed[1][z]

    @pl.when(core == 1)
    def _():
        for z in range(NZ):
            keep_ref[0, z] = packed[1][z]
            give_ref[0, z] = packed[0][z]


def part_products(where, right_owner, right_pick, half, right):
    out = jax.ShapeDtypeStruct((NY, NZ, NX * VECS * ROWS, B), jnp.bfloat16)
    smem = pl.BlockSpec(memory_space=pltpu.SMEM)
    out_block = pl.BlockSpec((1, NZ, NX * VECS * ROWS, B), lambda y: (y, 0, 0, 0))
    return pl.pallas_call(
        part_kernel,
        out_shape=(out, out),
        grid=(NY,),
        in_specs=[
            smem,
            smem,
            smem,
            pl.BlockSpec((1, NX, VECS * B, TERM_DEV * B), lambda y: (y, 0, 0, 0)),
            pl.BlockSpec((1, TERM_DEV * 2, B, B), lambda y: (y, 0, 0, 0)),
        ],
        out_specs=(out_block, out_block),
        scratch_shapes=[pltpu.SMEM((NX * NY + 1,), jnp.int32)],
        compiler_params=pltpu.CompilerParams(vmem_limit_bytes=32 * 1024 * 1024),
        cost_estimate=pl.CostEstimate(
            flops=2 * NY * NX * VECS * TERM_DEV * B**3, bytes_accessed=18 * 2**20, transcendentals=0
        ),
        name="part",
    )(where, right_owner, right_pick, half, right)


def shards(psi, left_env, right_env, left_pick, right_owner, right_pick):
    here = lax.axis_index("sec")
    where = jnp.stack([here, lax.axis_index("term") % 2]).astype(jnp.int32)
    rights = lax.all_gather(
        right_env.reshape(TERM_DEV * 2, B, B), "sec", axis=0, tiled=False, axis_index_groups=Y_GROUPS
    )
    psi_out, left_out = pack(where, right_owner, left_pick, psi, left_env.reshape(ENV_ROWS, B))
    own = lax.all_to_all(psi_out, "sec", 0, 0, tiled=True, axis_index_groups=X_GROUPS)
    other = lax.ppermute(own, "term", CORE_SWAP)
    left_out, own = lax.optimization_barrier((left_out, own))
    lefts = lax.all_to_all(left_out, "sec", 0, 0, tiled=True, axis_index_groups=X_GROUPS)
    half = half_products(where, own, other, lefts)
    keep, give = part_products(where, right_owner, right_pick, half, rights)
    got = lax.ppermute(give, "term", CORE_SWAP)
    both = (keep.astype(jnp.float32) + got.astype(jnp.float32)).astype(jnp.bfloat16)
    both = both.reshape(NY * NZ, NX * VECS * ROWS, B)
    arrived = lax.all_to_all(both, ("sec", "term"), 0, 0, tiled=True, axis_index_groups=YZ_GROUPS)
    arrived = arrived.reshape(NY, NZ, NX, VECS, ROWS, B)
    total = jnp.sum(arrived.astype(jnp.float32), axis=1)
    total = total.transpose(2, 0, 1, 3, 4).reshape(VECS, NY * NX, ROWS, B)
    valid = jnp.any(right_owner.reshape(-1, PAIR_DEV) == here, axis=1)
    return jnp.where(valid[None, :, None, None], total, 0.0).astype(jnp.bfloat16)


def solution(mesh):
    return jax.shard_map(
        shards,
        mesh=mesh,
        in_specs=(
            P(None, "sec", None, None),
            P("term", "sec", None, None),
            P("term", "sec", None, None),
            P("sec"),
            P(),
            P(),
        ),
        out_specs=P(None, "sec", "term", None),
        check_vma=False,
    )
```

time: 461 us -> 232 us (0.50)
  the two profiles are of different devices: /device:TPU:2 before, /device:TPU:16 now
where the time goes in v1:
time: 232 us; the launch traced here: 231 us
  Pallas kernels  94.2 us (41%)
  waiting for transfers between devices  45.3 us (20%)
  blocking collectives  43.8 us (19%)
  starting transfers between devices  20.4 us (9%)
  between operations  13.5 us (6%)
  local copies, waits for them, and re-layouts  10.8 us (5%)
  other arithmetic  3.32 us (1%)
    pallas_call x1, Pallas kernels, pack(): pl.pallas_call(pack_kernel, out_shape=(jax.ShapeDtypeStruct((NX, HALF_Y,...  81.8 us
    all_to_all x1, waiting for transfers between devices, shards(): lax.all_to_all(both, ('sec', 'term'), 0, 0, tiled=True, axis_index_groups...  41.2 us
    all_to_all x1, blocking collectives, shards(): lax.all_to_all(psi_out, 'sec', 0, 0, tiled=True, axis_index_groups=X_GROUPS)  25.1 us
    all_to_all x1, blocking collectives, shards(): lax.all_to_all(left_out, 'sec', 0, 0, tiled=True, axis_index_groups=X_GRO...  18.6 us
    all_to_all x1, starting transfers between devices, shards(): lax.all_to_all(both, ('sec', 'term'), 0, 0, tiled=True, axis_index_groups...  16.5 us
    unnamed x14, local copies, waits for them, and re-layouts  10.7 us
    pallas_call x1, Pallas kernels, part_products(): pl.pallas_call(part_kernel, out_shape=(out, out), grid=(NY,), in_specs=[s...  6.94 us
    pallas_call x1, Pallas kernels, half_products(): pl.pallas_call(half_kernel, out_shape=jax.ShapeDtypeStruct((NY, NX, VECS...  5.52 us
  transfers between devices with their start and end apart: 4, of which 2 were waited for; matrix products, arithmetic and copies ran while one was open for 0% of the time, Pallas kernels for 38%

profile of v1, /device:TPU:16, one launch (start us, length us, event | category | flops | bytes accessed | tf_op | source)
XLA Modules:
  0.0 231.3 jit_solution(4787072178305866592)
XLA Ops:
  6.5 0.0 all-gather.2.cloned.1.call-start
  6.5 0.7 all-gather.2.cloned.1.call-update
  7.3 0.6 pad_add_fusion.where_ref
  7.9 81.8 %pack.1 = (bf16[4,4,3,128,128]{4,3,2,1,0:T(8,128)(2,1)}, bf16[4,1040,128]{2,1,0:T(8,128)(2,1)}) custom-call(s32[2]{0:T(128)} %pad_add_fusion.where_ref, s32[512]{0:T(512)} %owner_ref.3, s32[16]{0:T(128)} %pick_ref.2, bf16[3,16,128,128]{3,2,1,0:T(8,128)(2,1)} %psi_ref.1, bf16[1024,128]{1,0:T(8,128)(2,1)} %bitcast.14), custom_call_target="tpu_custom_call" | custom-call | tf_op jit(solution)/shard_map/pack/pallas_call | solution.py:77
  89.7 0.0 copy-start.6
  89.7 25.1 %all_to_all.15.own_ref = bf16[4,4,3,128,128]{4,3,2,1,0:T(8,128)(2,1)S(1)} all-to-all(bf16[4,4,3,128,128]{4,3,2,1,0:T(8,128)(2,1)} %get-tuple-element.12), channel_id=1, replica_groups={{0,16,32,48},{64,80,96,112},{128,144,160,176},{192,208,224,240},{256,27..., dimensions={0} | all-to-all | bytes 3145728 | tf_op jit(solution)/shard_map/all_to_all | solution.py:239
  114.8 0.0 copy-start.4
  114.8 2.0 collective-permute-start
  116.9 0.0 copy-done.6
  116.9 18.6 %all_to_all.16.left_ref = bf16[4,1040,128]{2,1,0:T(8,128)(2,1)S(1)} all-to-all(bf16[4,1040,128]{2,1,0:T(8,128)(2,1)S(1)} %copy-done.6), channel_id=1, replica_groups={{0,16,32,48},{64,80,96,112},{128,144,160,176},{192,208,224,240},{256,27..., dimensions={0} | all-to-all | bytes 2129920 | tf_op jit(solution)/shard_map/all_to_all | solution.py:242
  135.5 0.0 copy-start.3
  135.5 0.0 copy-start.5
  135.5 0.0 collective-permute-done.other_ref
  135.5 0.0 copy-done.4
  135.5 5.5 %half.1.half_ref = bf16[8,4,384,512]{3,2,1,0:T(8,128)(2,1)S(1)} custom-call(s32[2]{0:T(128)S(1)} %copy-done.4, bf16[4,4,3,128,128]{4,3,2,1,0:T(8,128)(2,1)S(1)} %all_to_all.15.own_ref, bf16[4,4,3,128,128]{4,3,2,1,0:T(8,128)(2,1)S(1)} %collective-permute-done.other_ref, bf16[4,1040,128]{2,1,0:T(8,128)(2,1)S(1)} %all_to_all.16.left_ref), custom_call_target="tpu_custom_call" | custom-call | flops 1610612736 | bytes 17825792 | tf_op jit(solution)/shard_map/half/pallas_call | solution.py:134
  141.0 0.0 copy-start
  141.0 4.5 %copy-done = bf16[8,4,384,512]{3,2,1,0:T(8,128)(2,1)} copy-done((bf16[8,4,384,512]{3,2,1,0:T(8,128)(2,1)}, bf16[8,4,384,512]{3,2,1,0:T(8,128)(2,1)S(1)}, u32[]{:S(2)}) %copy-start) | copy-done | bytes 12582936
  145.6 0.0 all-gather.2.cloned.1.call-done.right_ref
  145.6 0.0 copy-done.3
  145.6 0.0 copy-done.5
  145.6 0.0 copy-start.1
  145.6 4.6 %copy-done.1 = bf16[8,4,384,512]{3,2,1,0:T(8,128)(2,1)S(1)} copy-done((bf16[8,4,384,512]{3,2,1,0:T(8,128)(2,1)S(1)}, bf16[8,4,384,512]{3,2,1,0:T(8,128)(2,1)}, u32[]{:S(2)}) %copy-start.1) | copy-done | bytes 12582936
  150.2 0.0 copy-start.2
  150.2 1.6 copy-done.2
  151.7 6.9 %part.1 = (bf16[8,8,96,128]{3,2,1,0:T(8,128)(2,1)S(1)}, bf16[8,8,96,128]{3,2,1,0:T(8,128)(2,1)S(1)}) custom-call(s32[2]{0:T(128)S(1)} %copy-done.4, s32[512]{0:T(512)S(1)} %copy-done.3, s32[512]{0:T(512)S(1)} %copy-done.5, bf16[8,4,384,512]{3,2,1,0:T(8,128)(2,1)S(1)} %copy-done.1, bf16[8,8,128,128]{3,2,1,0:T(8,128)(2,1)S(1)} %copy-done.2), custom_call_target="tpu_custom_call" | custom-call | flops 1610612736 | bytes 18874368 | tf_op jit(solution)/shard_map/part/pallas_call | solution.py:211
  158.7 1.9 collective-permute-start.1
  160.6 3.4 %collective-permute-done.1 = bf16[8,8,96,128]{3,2,1,0:T(8,128)(2,1)S(1)} collective-permute-done((bf16[8,8,96,128]{3,2,1,0:T(8,128)(2,1)S(1)}, bf16[8,8,96,128]{3,2,1,0:T(8,128)(2,1)S(1)}, u32[]{:S(2)}, u32[]{:S(2)}) %collective-permute-start.1) | collective-permute-done | bytes 1572896 | tf_op jit(solution)/shard_map/ppermute | solution.py:245
  164.0 1.6 add_convert_fusion
  165.6 16.5 %all-to-all-start.2 = ((bf16[64,96,128]{2,1,0:T(8,128)(2,1)}), bf16[64,96,128]{2,1,0:T(8,128)(2,1)S(1)}, u32[]{:S(2)}, u32[]{:S(2)}) async-start(bf16[64,96,128]{2,1,0:T(8,128)(2,1)} %bitcast.4), calls=%async_computation.2 | async-start | bytes 3145728 | tf_op jit(solution)/shard_map/all_to_all | solution.py:248
  182.1 0.1 eq.13
  182.2 0.1 reduce_or.9
  182.3 41.2 %all-to-all-done.2 = bf16[64,96,128]{2,1,0:T(8,128)(2,1)S(1)} async-done(((bf16[64,96,128]{2,1,0:T(8,128)(2,1)}), bf16[64,96,128]{2,1,0:T(8,128)(2,1)S(1)}, u32[]{:S(2)}, u32[]{:S(2)}) %all-to-all-start.2) | async-done | bytes 1572896 | tf_op jit(solution)/shard_map/all_to_all | solution.py:248
  223.5 0.2 convert_reduce_fusion
  223.7 0.8 fusion
  (1 shorter events, 0.0 us)
Async XLA Ops:
  6.5 139.0 %all-gather.2.cloned.1.call-start = ((), (), s32[]{:S(2)}) async-start(), calls=%async_computation.3 | async-start | bytes 2359296 | tf_op jit(solution)/shard_map/all_gather | solution.py:235
  89.7 27.2 %copy-start.6 = (bf16[4,1040,128]{2,1,0:T(8,128)(2,1)S(1)}, bf16[4,1040,128]{2,1,0:T(8,128)(2,1)}, u32[]{:S(2)}) copy-start(bf16[4,1040,128]{2,1,0:T(8,128)(2,1)} %get-tuple-element.14) | copy-start | bytes 3194884
  114.8 20.7 %copy-start.4 = (s32[2]{0:T(128)S(1)}, s32[2]{0:T(128)}, u32[]{:S(2)}) copy-start(s32[2]{0:T(128)} %pad_add_fusion.where_ref) | copy-start | bytes 28
  114.8 20.7 %collective-permute-start = (bf16[4,4,3,128,128]{4,3,2,1,0:T(8,128)(2,1)S(1)}, bf16[4,4,3,128,128]{4,3,2,1,0:T(8,128)(2,1)S(1)}, u32[]{:S(2)}, u32[]{:S(2)}) collective-permute-start(bf16[4,4,3,128,128]{4,3,2,1,0:T(8,128)(2,1)S(1)} %all_to_all.15.own_ref), channel_id=1, source_target_pairs={{0,1},{1,0},{2,3},{3,2},{4,5},{5,4},{6,7},{7,6},{8,9},{9,8},{10,11... | collective-permute-start | bytes 4718600 | tf_op jit(solution)/shard_map/ppermute | solution.py:240
  135.5 10.1 %copy-start.3 = (s32[512]{0:T(512)S(1)}, s32[512]{0:T(512)}, u32[]{:S(2)}) copy-start(s32[512]{0:T(512)} %owner_ref.3) | copy-start | bytes 6148
  135.5 10.1 %copy-start.5 = (s32[512]{0:T(512)S(1)}, s32[512]{0:T(512)}, u32[]{:S(2)}) copy-start(s32[512]{0:T(512)} %pick_ref.3) | copy-start | bytes 6148
  141.0 4.5 %copy-start = (bf16[8,4,384,512]{3,2,1,0:T(8,128)(2,1)}, bf16[8,4,384,512]{3,2,1,0:T(8,128)(2,1)S(1)}, u32[]{:S(2)}) copy-start(bf16[8,4,384,512]{3,2,1,0:T(8,128)(2,1)S(1)} %half.1.half_ref) | copy-start | bytes 37748740
  145.6 4.6 %copy-start.1 = (bf16[8,4,384,512]{3,2,1,0:T(8,128)(2,1)S(1)}, bf16[8,4,384,512]{3,2,1,0:T(8,128)(2,1)}, u32[]{:S(2)}) copy-start(bf16[8,4,384,512]{3,2,1,0:T(8,128)(2,1)} %copy-done) | copy-start | bytes 37748740
  150.2 1.6 copy-start.2
  158.7 5.3 %collective-permute-start.1 = (bf16[8,8,96,128]{3,2,1,0:T(8,128)(2,1)S(1)}, bf16[8,8,96,128]{3,2,1,0:T(8,128)(2,1)S(1)}, u32[]{:S(2)}, u32[]{:S(2)}) collective-permute-start(bf16[8,8,96,128]{3,2,1,0:T(8,128)(2,1)S(1)} %get-tuple-element.16), channel_id=1, source_target_pairs={{0,1},{1,0},{2,3},{3,2},{4,5},{5,4},{6,7},{7,6},{8,9},{9,8},{10,11... | collective-permute-start | bytes 4718600 | tf_op jit(solution)/shard_map/ppermute | solution.py:245
  165.6 57.9 %all-to-all-start.2 = ((bf16[64,96,128]{2,1,0:T(8,128)(2,1)}), bf16[64,96,128]{2,1,0:T(8,128)(2,1)S(1)}, u32[]{:S(2)}, u32[]{:S(2)}) async-start(bf16[64,96,128]{2,1,0:T(8,128)(2,1)} %bitcast.4), calls=%async_computation.2 | async-start | bytes 3145728 | tf_op jit(solution)/shard_map/all_to_all | solution.py:248
Sparse Core Ops, SparseCore 0:
  9.4 88.2 all-gather.1

commit v2 on v0

v2 whole, which is shorter than its diff:
```python
import jax
import jax.numpy as jnp
from jax import lax
from jax.experimental import pallas as pl
from jax.experimental.pallas import tpu as pltpu
from jax.sharding import PartitionSpec as P

B = 128
VECS = 3
PAIR_DEV = 16
TERM_DEV = 4
NX = 4
NY = 8
NZ = 8
HALF_Y = NY // 2
ENV_ROWS = TERM_DEV * 2 * B
PICK_ROWS = 16
PSI_ROWS = HALF_Y * VECS * B
SENT_ROWS = PSI_ROWS + ENV_ROWS + PICK_ROWS
ROWS = 8

X_GROUPS = [[y * NX + x for x in range(NX)] for y in range(NY)]
Y_GROUPS = [[y * NX + x for y in range(NY)] for x in range(NX)]
YZ_GROUPS = [
    [(y * NX + x) * 2 * NZ + z * 2 + c for y in range(NY) for z in range(NZ)]
    for x in range(NX)
    for c in range(2)
]
CORE_SWAP = [(z * 2 + c, z * 2 + 1 - c) for z in range(NZ) for c in range(2)]


def pack_kernel(where_ref, owner_ref, pick_ref, psi_ref, left_ref, out_ref, table, sems):
    here, core = where_ref[0], where_ref[1]

    def clear(i, _):
        table[i] = 0
        return 0

    lax.fori_loop(0, NX * NY, clear, 0)

    def fill(j, _):
        table[owner_ref[here * PAIR_DEV + j]] = j
        return 0

    lax.fori_loop(0, PAIR_DEV, fill, 0)
    copies = []
    for x in range(NX):
        for i in range(HALF_Y):
            src = table[(core * HALF_Y + i) * NX + x]
            for v in range(VECS):
                copies.append(
                    pltpu.make_async_copy(
                        psi_ref.at[v, src],
                        out_ref.at[x, pl.ds((i * VECS + v) * B, B)],
                        sems.at[len(copies)],
                    )
                )
        copies.append(
            pltpu.make_async_copy(
                left_ref, out_ref.at[x, pl.ds(PSI_ROWS, ENV_ROWS)], sems.at[len(copies)]
            )
        )
    for copy in copies:
        copy.start()
    row = lax.broadcasted_iota(jnp.int32, (PICK_ROWS, B), 0)
    for x in range(NX):
        value = jnp.zeros((PICK_ROWS, B), jnp.int32)
        for y in range(NY):
            value = jnp.where(row == y, pick_ref[table[y * NX + x]], value)
        out_ref[x, pl.ds(PSI_ROWS + ENV_ROWS, PICK_ROWS)] = value.astype(jnp.float32).astype(jnp.bfloat16)
    for copy in copies:
        copy.wait()


def pack(where, right_owner, left_pick, psi, left):
    smem = pl.BlockSpec(memory_space=pltpu.SMEM)
    hbm = pl.BlockSpec(memory_space=pl.ANY)
    return pl.pallas_call(
        pack_kernel,
        out_shape=jax.ShapeDtypeStruct((NX, SENT_ROWS, B), jnp.bfloat16),
        in_specs=[smem, smem, smem, hbm, hbm],
        out_specs=pl.BlockSpec(memory_space=pltpu.VMEM),
        scratch_shapes=[
            pltpu.SMEM((NX * NY,), jnp.int32),
            pltpu.SemaphoreType.DMA((NX * (HALF_Y * VECS + 1),)),
        ],
        compiler_params=pltpu.CompilerParams(vmem_limit_bytes=32 * 1024 * 1024),
        name="pack",
    )(where, right_owner, left_pick, psi, left)


def part_kernel(
    where_ref, owner_ref, pick_ref, got_ref, other_ref, right_ref, keep_ref, give_ref, table
):
    group, i = pl.program_id(0), pl.program_id(1)
    here, core = where_ref[0], where_ref[1]
    my_y, my_x = here // NX, here % NX
    right_y = ((group + core) % 2) * HALF_Y + i

    @pl.when((group == 0) & (i == 0))
    def _():
        def clear(k, _):
            table[k] = 0
            return 0

        lax.fori_loop(0, NX * NY, clear, 0)

        def fill(j, _):
            block = my_y * NX * PAIR_DEV + j
            owner = owner_ref[block]
            slot = jnp.where(owner % NX == my_x, (j // PAIR_DEV) * NY + owner // NX, NX * NY)
            table[slot] = pick_ref[block]
            return 0

        lax.fori_loop(0, NX * PAIR_DEV, fill, 0)

    def work(load_psi):
        row = lax.broadcasted_iota(jnp.int32, (PICK_ROWS, B), 0)
        groups = [[[] for _ in range(NZ)] for _ in range(2)]
        for x in range(NX):
            picks = got_ref[x, pl.ds(PSI_ROWS + ENV_ROWS, PICK_ROWS), :].astype(jnp.float32)
            second = jnp.max(jnp.where(row == right_y, picks, 0.0), axis=0, keepdims=True) > 0.5
            second = jnp.broadcast_to(second, (B, B))
            lefts = []
            for t in range(TERM_DEV):
                first_env = got_ref[x, pl.ds(PSI_ROWS + (t * 2) * B, B), :]
                second_env = got_ref[x, pl.ds(PSI_ROWS + (t * 2 + 1) * B, B), :]
                lefts.append(jnp.where(second, second_env, first_env))
            lefts = jnp.concatenate(lefts, axis=0)
            vecs = jnp.concatenate([load_psi(x, v) for v in range(VECS)], axis=1)
            half = jnp.dot(lefts, vecs, preferred_element_type=jnp.float32).astype(jnp.bfloat16)
            half = jnp.concatenate(
                [
                    jnp.concatenate(
                        [half[t * B : (t + 1) * B, v * B : (v + 1) * B] for t in range(TERM_DEV)], axis=1
                    )
                    for v in range(VECS)
                ],
                axis=0,
            )
            pick = table[x * NY + right_y]
            rights = jnp.concatenate([right_ref[0, t * 2 + pick] for t in range(TERM_DEV)], axis=0)
            prod = jnp.dot(half, rights, preferred_element_type=jnp.float32)
            for v in range(VECS):
                for z in range(NZ):
                    for c in range(2):
                        at = v * B + (z * 2 + c) * ROWS
                        groups[c][z].append(prod[at : at + ROWS])
        packed = [
            [jnp.concatenate(groups[c][z], axis=0).astype(jnp.bfloat16) for z in range(NZ)]
            for c in range(2)
        ]

        @pl.when(core == 0)
        def _():
            for z in range(NZ):
                keep_ref[0, z] = packed[0][z]
                give_ref[0, z] = packed[1][z]

        @pl.when(core == 1)
        def _():
            for z in range(NZ):
                keep_ref[0, z] = packed[1][z]
                give_ref[0, z] = packed[0][z]

    @pl.when(group == 0)
    def _():
        work(lambda x, v: got_ref[x, pl.ds(pl.multiple_of(i * VECS * B, B) + v * B, B), :])

    @pl.when(group == 1)
    def _():
        work(lambda x, v: other_ref[x, pl.ds(v * B, B), :])


def part_products(where, right_owner, right_pick, got, other, right):
    out = jax.ShapeDtypeStruct((NY, NZ, NX * VECS * ROWS, B), jnp.bfloat16)
    smem = pl.BlockSpec(memory_space=pltpu.SMEM)

    def right_y(g, i, where_ref):
        return ((g + where_ref[1]) % 2) * HALF_Y + i

    out_block = pl.BlockSpec(
        (1, NZ, NX * VECS * ROWS, B), lambda g, i, where_ref: (right_y(g, i, where_ref), 0, 0, 0)
    )
    return pl.pallas_call(
        part_kernel,
        out_shape=(out, out),
        grid_spec=pltpu.PrefetchScalarGridSpec(
            num_scalar_prefetch=1,
            grid=(2, HALF_Y),
            in_specs=[
                smem,
                smem,
                pl.BlockSpec((NX, SENT_ROWS, B), lambda g, i, where_ref: (0, 0, 0)),
                pl.BlockSpec((NX, VECS * B, B), lambda g, i, where_ref: (0, g * i, 0)),
                pl.BlockSpec(
                    (1, TERM_DEV * 2, B, B),
                    lambda g, i, where_ref: (right_y(g, i, where_ref), 0, 0, 0),
                ),
            ],
            out_specs=(out_block, out_block),
            scratch_shapes=[pltpu.SMEM((NX * NY + 1,), jnp.int32)],
        ),
        compiler_params=pltpu.CompilerParams(vmem_limit_bytes=32 * 1024 * 1024),
        cost_estimate=pl.CostEstimate(
            flops=4 * NY * NX * VECS * TERM_DEV * B**3, bytes_accessed=10 * 2**20, transcendentals=0
        ),
        name="part",
    )(where, right_owner, right_pick, got, other, right)


def shards(psi, left_env, right_env, left_pick, right_owner, right_pick):
    here = lax.axis_index("sec")
    where = jnp.stack([here, lax.axis_index("term") % 2]).astype(jnp.int32)
    rights = lax.all_gather(
        right_env.reshape(TERM_DEV * 2, B, B), "sec", axis=0, tiled=False, axis_index_groups=Y_GROUPS
    )
    valid = jnp.any(right_owner.reshape(-1, PAIR_DEV) == here, axis=1)
    sent = pack(where, right_owner, left_pick, psi, left_env.reshape(ENV_ROWS, B))
    got = lax.all_to_all(sent, "sec", 0, 0, tiled=True, axis_index_groups=X_GROUPS)
    other = lax.ppermute(got[:, :PSI_ROWS], "term", CORE_SWAP)
    keep, give = part_products(where, right_owner, right_pick, got, other, rights)
    taken = lax.ppermute(give, "term", CORE_SWAP)
    both = (keep.astype(jnp.float32) + taken.astype(jnp.float32)).astype(jnp.bfloat16)
    both = both.reshape(NY * NZ, NX * VECS * ROWS, B)
    both, valid = lax.optimization_barrier((both, valid))
    arrived = lax.all_to_all(both, ("sec", "term"), 0, 0, tiled=True, axis_index_groups=YZ_GROUPS)
    arrived = arrived.reshape(NY, NZ, NX, VECS, ROWS, B)
    total = jnp.sum(arrived.astype(jnp.float32), axis=1)
    total = total.transpose(2, 0, 1, 3, 4).reshape(VECS, NY * NX, ROWS, B)
    return jnp.where(valid[None, :, None, None], total, 0.0).astype(jnp.bfloat16)


def solution(mesh):
    return jax.shard_map(
        shards,
        mesh=mesh,
        in_specs=(
            P(None, "sec", None, None),
            P("term", "sec", None, None),
            P("term", "sec", None, None),
            P("sec"),
            P(),
            P(),
        ),
        out_specs=P(None, "sec", "term", None),
        check_vma=False,
    )
```

time: 461 us -> 149 us (0.32)
  the two profiles are of different devices: /device:TPU:2 before, /device:TPU:16 now
where the time goes in v2:
time: 149 us; the launch traced here: 148 us
  blocking collectives  93.9 us (63%)
  Pallas kernels  17.3 us (12%)
  between operations  13.5 us (9%)
  local copies, waits for them, and re-layouts  9.21 us (6%)
  waiting for transfers between devices  7.33 us (5%)
  starting transfers between devices  3.96 us (3%)
  other arithmetic  3.02 us (2%)
    all_to_all x1, blocking collectives, shards(): lax.all_to_all(both, ('sec', 'term'), 0, 0, tiled=True, axis_index_groups...  57.7 us
    all_to_all x1, blocking collectives, shards(): lax.all_to_all(sent, 'sec', 0, 0, tiled=True, axis_index_groups=X_GROUPS)  36.2 us
    pallas_call x1, Pallas kernels, part_products(): pl.pallas_call(part_kernel, out_shape=(out, out), grid_spec=pltpu.Prefetc...  13.7 us
    unnamed x20, local copies, waits for them, and re-layouts  9.02 us
    pallas_call x1, Pallas kernels, pack(): pl.pallas_call(pack_kernel, out_shape=jax.ShapeDtypeStruct((NX, SENT_ROWS...  3.67 us
    ppermute x1, waiting for transfers between devices, shards(): other = lax.ppermute(got[:, :PSI_ROWS], 'term', CORE_SWAP)  3.38 us
    ppermute x1, waiting for transfers between devices, shards(): taken = lax.ppermute(give, 'term', CORE_SWAP)  3.24 us
  transfers between devices with their start and end apart: 3, of which 2 were waited for; matrix products, arithmetic and copies ran while one was open for 0% of the time, Pallas kernels for 2%

profile of v2, /device:TPU:16, one launch (start us, length us, event | category | flops | bytes accessed | tf_op | source)
XLA Modules:
  0.0 148.2 jit_solution(4508199775318391917)
XLA Ops:
  6.5 0.0 all-gather.2.cloned.1.call-start
  6.5 0.7 all-gather.2.cloned.1.call-update
  7.3 0.1 pad_add_fusion.where_ref
  7.3 0.0 copy-start
  7.3 1.4 copy-done
  8.8 0.0 copy-start.2
  8.8 0.9 copy-done.2
  9.7 0.0 copy-start.3
  9.7 0.7 copy-done.3
  10.4 0.0 copy-start.5
  10.4 0.7 copy-done.5
  11.0 3.7 %pack.1 = bf16[4,2576,128]{2,1,0:T(8,128)(2,1)S(1)} custom-call(s32[2]{0:T(128)S(1)} %pad_add_fusion.where_ref, s32[512]{0:T(512)S(1)} %copy-done.3, s32[16]{0:T(128)S(1)} %copy-done.5, bf16[3,16,128,128]{3,2,1,0:T(8,128)(2,1)S(1)} %copy-done, bf16[1024,128]{1,0:T(8,128)(2,1)S(1)} %bitcast.12), custom_call_target="tpu_custom_call" | custom-call | tf_op jit(solution)/shard_map/pack/pallas_call | solution.py:78
  14.7 36.2 %all_to_all.10.got_ref = bf16[4,2576,128]{2,1,0:T(8,128)(2,1)S(1)} all-to-all(bf16[4,2576,128]{2,1,0:T(8,128)(2,1)S(1)} %pack.1), channel_id=1, replica_groups={{0,16,32,48},{64,80,96,112},{128,144,160,176},{192,208,224,240},{256,27..., dimensions={0} | all-to-all | bytes 5275648 | tf_op jit(solution)/shard_map/all_to_all | solution.py:220
  50.9 0.0 copy-start.4
  50.9 0.0 copy-start.9
  50.9 0.1 slice.4
  51.0 1.9 %collective-permute-start = (bf16[4,1536,128]{2,1,0:T(8,128)(2,1)S(1)}, bf16[4,1536,128]{2,1,0:T(8,128)(2,1)S(1)}, u32[]{:S(2)}, u32[]{:S(2)}) collective-permute-start(bf16[4,1536,128]{2,1,0:T(8,128)(2,1)S(1)} %slice.4), channel_id=1, source_target_pairs={{0,1},{1,0},{2,3},{3,2},{4,5},{5,4},{6,7},{7,6},{8,9},{9,8},{10,11... | collective-permute-start | bytes 4718600 | tf_op jit(solution)/shard_map/ppermute | solution.py:221
  53.0 3.4 %collective-permute-done.other_ref = bf16[4,1536,128]{2,1,0:T(8,128)(2,1)S(1)} collective-permute-done((bf16[4,1536,128]{2,1,0:T(8,128)(2,1)S(1)}, bf16[4,1536,128]{2,1,0:T(8,128)(2,1)S(1)}, u32[]{:S(2)}, u32[]{:S(2)}) %collective-permute-start) | collective-permute-done | bytes 1572896 | tf_op jit(solution)/shard_map/ppermute | solution.py:221
  56.3 0.0 copy-start.7
  56.3 1.2 copy-done.7
  57.5 0.0 all-gather.2.cloned.1.call-done.right_ref
  57.5 0.0 copy-done.4
  57.5 0.0 copy-done.9
  57.5 0.0 copy-start.6
  57.5 1.6 %copy-done.6 = bf16[8,8,128,128]{3,2,1,0:T(8,128)(2,1)S(1)} copy-done((bf16[8,8,128,128]{3,2,1,0:T(8,128)(2,1)S(1)}, bf16[8,8,128,128]{3,2,1,0:T(8,128)(2,1)}, u32[]{:S(2)}) %copy-start.6) | copy-done | bytes 2097176
  59.1 0.0 copy-start.8
  59.1 1.4 copy-done.8
  60.5 13.7 %part.1 = (bf16[8,8,96,128]{3,2,1,0:T(8,128)(2,1)S(1)}, bf16[8,8,96,128]{3,2,1,0:T(8,128)(2,1)}) custom-call(s32[2]{0:T(128)S(1)} %pad_add_fusion.where_ref, s32[512]{0:T(512)S(1)} %copy-done.4, s32[512]{0:T(512)S(1)} %copy-done.9, bf16[4,2576,128]{2,1,0:T(8,128)(2,1)S(1)} %all_to_all.10.got_ref, bf16[4,1536,128]{2,1,0:T(8,128)(2,1)S(1)} %copy-done.8, ...), custom_call_target="tpu_custom_call" | custom-call | flops 3221225472 | bytes 10485760 | tf_op jit(solution)/shard_map/part/pallas_call | solution.py:185
  74.2 0.0 copy-start.1
  74.2 1.2 copy-done.1
  75.4 2.0 %collective-permute-start.1 = (bf16[8,8,96,128]{3,2,1,0:T(8,128)(2,1)}, bf16[8,8,96,128]{3,2,1,0:T(8,128)(2,1)S(1)}, u32[]{:S(2)}, u32[]{:S(2)}) collective-permute-start(bf16[8,8,96,128]{3,2,1,0:T(8,128)(2,1)} %get-tuple-element.10), channel_id=1, source_target_pairs={{0,1},{1,0},{2,3},{3,2},{4,5},{5,4},{6,7},{7,6},{8,9},{9,8},{10,11... | collective-permute-start | bytes 4718600 | tf_op jit(solution)/shard_map/ppermute | solution.py:223
  77.4 0.1 eq.13
  77.5 0.1 reduce_or.9
  77.6 3.2 %collective-permute-done.1 = bf16[8,8,96,128]{3,2,1,0:T(8,128)(2,1)S(1)} collective-permute-done((bf16[8,8,96,128]{3,2,1,0:T(8,128)(2,1)}, bf16[8,8,96,128]{3,2,1,0:T(8,128)(2,1)S(1)}, u32[]{:S(2)}, u32[]{:S(2)}) %collective-permute-start.1) | collective-permute-done | bytes 1572896 | tf_op jit(solution)/shard_map/ppermute | solution.py:223
  80.9 1.8 %add_convert_fusion = bf16[8,8,96,128]{3,2,1,0:T(8,128)(2,1)S(1)} fusion(bf16[8,8,96,128]{3,2,1,0:T(8,128)(2,1)S(1)} %collective-permute-done.1, bf16[8,8,96,128]{3,2,1,0:T(8,128)(2,1)} %copy-done.1), kind=kLoop, calls=%fused_computation.1 | loop fusion | flops 3145728 | bytes 4718592 | tf_op jit(solution)/shard_map/convert_element_type | solution.py:224
  82.7 57.7 %all_to_all.11 = bf16[64,96,128]{2,1,0:T(8,128)(2,1)S(1)} all-to-all(bf16[64,96,128]{2,1,0:T(8,128)(2,1)S(1)} %bitcast.14), channel_id=1, replica_groups={{0,2,4,6,8,10,12,14,64,66,68,70,72,74,76,78,128,130,132,134,136,138,140..., dimensions={0} | all-to-all | bytes 3145728 | tf_op jit(solution)/shard_map/all_to_all | solution.py:227
  140.4 0.2 convert_reduce_fusion
  140.6 0.8 fusion
  (1 shorter events, 0.0 us)
Async XLA Ops:
  6.5 51.0 %all-gather.2.cloned.1.call-start = ((), (), s32[]{:S(2)}) async-start(), calls=%async_computation.2 | async-start | bytes 2359296 | tf_op jit(solution)/shard_map/all_gather | solution.py:215
  7.3 1.4 copy-start
  8.8 0.9 copy-start.2
  9.7 0.7 copy-start.3
  10.4 0.7 copy-start.5
  50.9 6.6 %copy-start.4 = (s32[512]{0:T(512)S(1)}, s32[512]{0:T(512)}, u32[]{:S(2)}) copy-start(s32[512]{0:T(512)} %owner_ref.3) | copy-start | bytes 6148
  50.9 6.6 %copy-start.9 = (s32[512]{0:T(512)S(1)}, s32[512]{0:T(512)}, u32[]{:S(2)}) copy-start(s32[512]{0:T(512)} %pick_ref.3) | copy-start | bytes 6148
  51.0 5.3 %collective-permute-start = (bf16[4,1536,128]{2,1,0:T(8,128)(2,1)S(1)}, bf16[4,1536,128]{2,1,0:T(8,128)(2,1)S(1)}, u32[]{:S(2)}, u32[]{:S(2)}) collective-permute-start(bf16[4,1536,128]{2,1,0:T(8,128)(2,1)S(1)} %slice.4), channel_id=1, source_target_pairs={{0,1},{1,0},{2,3},{3,2},{4,5},{5,4},{6,7},{7,6},{8,9},{9,8},{10,11... | collective-permute-start | bytes 4718600 | tf_op jit(solution)/shard_map/ppermute | solution.py:221
  56.3 1.2 copy-start.7
  57.5 1.6 %copy-start.6 = (bf16[8,8,128,128]{3,2,1,0:T(8,128)(2,1)S(1)}, bf16[8,8,128,128]{3,2,1,0:T(8,128)(2,1)}, u32[]{:S(2)}) copy-start(bf16[8,8,128,128]{3,2,1,0:T(8,128)(2,1)} %all-gather.2.cloned.1.call-done.right_ref) | copy-start | bytes 6291460
  59.1 1.4 copy-start.8
  74.2 1.2 copy-start.1
  75.4 5.5 %collective-permute-start.1 = (bf16[8,8,96,128]{3,2,1,0:T(8,128)(2,1)}, bf16[8,8,96,128]{3,2,1,0:T(8,128)(2,1)S(1)}, u32[]{:S(2)}, u32[]{:S(2)}) collective-permute-start(bf16[8,8,96,128]{3,2,1,0:T(8,128)(2,1)} %get-tuple-element.10), channel_id=1, source_target_pairs={{0,1},{1,0},{2,3},{3,2},{4,5},{5,4},{6,7},{7,6},{8,9},{9,8},{10,11... | collective-permute-start | bytes 4718600 | tf_op jit(solution)/shard_map/ppermute | solution.py:223
Sparse Core Ops, SparseCore 0:
  9.4 47.1 all-gather.1

commit v3 on v2

v3 whole, which is shorter than its diff:
```python
import jax
import jax.numpy as jnp
from jax import lax
from jax.experimental import pallas as pl
from jax.experimental.pallas import tpu as pltpu
from jax.sharding import PartitionSpec as P

B = 128
VECS = 3
PAIR_DEV = 16
TERM_DEV = 4
NX = 4
NY = 8
NZ = 8
HALF_Y = NY // 2
ENV_ROWS = TERM_DEV * 2 * B
PICK_ROWS = 16
PSI_ROWS = HALF_Y * VECS * B
SENT_ROWS = PSI_ROWS + ENV_ROWS + PICK_ROWS
ROWS = 8

X_GROUPS = [[y * NX + x for x in range(NX)] for y in range(NY)]
Y_GROUPS = [[y * NX + x for y in range(NY)] for x in range(NX)]
YZ_GROUPS = [
    [((y + c * HALF_Y) % NY * NX + x) * 2 * NZ + z * 2 + c for y in range(NY) for z in range(NZ)]
    for x in range(NX)
    for c in range(2)
]
CORE_SWAP = [(z * 2 + c, z * 2 + 1 - c) for z in range(NZ) for c in range(2)]


def pack_kernel(where_ref, owner_ref, pick_ref, psi_ref, left_ref, out_ref, table, sems):
    here, core = where_ref[0], where_ref[1]

    def clear(i, _):
        table[i] = 0
        return 0

    lax.fori_loop(0, NX * NY, clear, 0)

    def fill(j, _):
        table[owner_ref[here * PAIR_DEV + j]] = j
        return 0

    lax.fori_loop(0, PAIR_DEV, fill, 0)
    copies = []
    for x in range(NX):
        for i in range(HALF_Y):
            src = table[(core * HALF_Y + i) * NX + x]
            for v in range(VECS):
                copies.append(
                    pltpu.make_async_copy(
                        psi_ref.at[v, src],
                        out_ref.at[x, pl.ds((i * VECS + v) * B, B)],
                        sems.at[len(copies)],
                    )
                )
        copies.append(
            pltpu.make_async_copy(
                left_ref, out_ref.at[x, pl.ds(PSI_ROWS, ENV_ROWS)], sems.at[len(copies)]
            )
        )
    for copy in copies:
        copy.start()
    row = lax.broadcasted_iota(jnp.int32, (PICK_ROWS, B), 0)
    for x in range(NX):
        value = jnp.zeros((PICK_ROWS, B), jnp.int32)
        for y in range(NY):
            value = jnp.where(row == y, pick_ref[table[y * NX + x]], value)
        out_ref[x, pl.ds(PSI_ROWS + ENV_ROWS, PICK_ROWS)] = value.astype(jnp.float32).astype(jnp.bfloat16)
    for copy in copies:
        copy.wait()


def pack(where, right_owner, left_pick, psi, left):
    smem = pl.BlockSpec(memory_space=pltpu.SMEM)
    hbm = pl.BlockSpec(memory_space=pl.ANY)
    return pl.pallas_call(
        pack_kernel,
        out_shape=jax.ShapeDtypeStruct((NX, SENT_ROWS, B), jnp.bfloat16),
        in_specs=[smem, smem, smem, hbm, hbm],
        out_specs=pl.BlockSpec(memory_space=pltpu.VMEM),
        scratch_shapes=[
            pltpu.SMEM((NX * NY,), jnp.int32),
            pltpu.SemaphoreType.DMA((NX * (HALF_Y * VECS + 1),)),
        ],
        name="pack",
    )(where, right_owner, left_pick, psi, left)


def part_kernel(mine, where_ref, owner_ref, pick_ref, got_ref, psi_ref, right_ref, keep_ref, give_ref, table, rows):
    i = pl.program_id(0)
    core = where_ref[1]
    right_y = (core if mine else 1 - core) * HALF_Y + i

    @pl.when(i == 0)
    def _():
        here = where_ref[0]
        my_x = here & (NX - 1)
        first = (here - my_x) * PAIR_DEV

        for k in range(NX * NY):
            table[k] = 0

        def fill(j, _):
            owner = owner_ref[first + j]
            slot = lax.shift_right_logical(j, 4) * NY + lax.shift_right_logical(owner, 2)
            table[jnp.where((owner & (NX - 1)) == my_x, slot, NX * NY)] = pick_ref[first + j]
            return 0

        lax.fori_loop(0, NX * PAIR_DEV, fill, 0, unroll=8)

    row = lax.broadcasted_iota(jnp.int32, (PICK_ROWS, B), 0)
    groups = [[[] for _ in range(NZ)] for _ in range(2)]
    for x in range(NX):
        picks = got_ref[x, pl.ds(PSI_ROWS + ENV_ROWS, PICK_ROWS), :].astype(jnp.float32)
        second = jnp.max(jnp.where(row == right_y, picks, 0.0), axis=0, keepdims=True) > 0.5
        second = jnp.broadcast_to(second, (B, B))
        lefts = []
        for t in range(TERM_DEV):
            first_env = got_ref[x, pl.ds(PSI_ROWS + (t * 2) * B, B), :]
            second_env = got_ref[x, pl.ds(PSI_ROWS + (t * 2 + 1) * B, B), :]
            lefts.append(jnp.where(second, second_env, first_env))
        lefts = jnp.concatenate(lefts, axis=0)
        pick = table[x * NY + right_y]
        rights = jnp.concatenate([right_ref[0, t * 2 + pick] for t in range(TERM_DEV)], axis=0)
        for v in range(VECS):
            if mine:
                vec = psi_ref[x, pl.ds(pl.multiple_of(i * VECS * B, B) + v * B, B), :]
            else:
                vec = psi_ref[x, pl.ds(v * B, B), :]
            half = jnp.dot(lefts, vec, preferred_element_type=jnp.float32).astype(jnp.bfloat16)
            half = jnp.concatenate([half[t * B : (t + 1) * B] for t in range(TERM_DEV)], axis=1)
            prod = jnp.dot(half, rights, preferred_element_type=jnp.float32)
            for z in range(NZ):
                for c in range(2):
                    at = (z * 2 + c) * ROWS
                    groups[c][z].append(prod[at : at + ROWS])
    for c in range(2):
        for z in range(NZ):
            rows[core ^ c, z] = jnp.concatenate(groups[c][z], axis=0).astype(jnp.bfloat16)
    keep_ref[0] = rows[0]
    give_ref[0] = rows[1]


def part_products(mine, where, right_owner, right_pick, got, psi, right):
    out = jax.ShapeDtypeStruct((HALF_Y, NZ, NX * VECS * ROWS, B), jnp.bfloat16)
    smem = pl.BlockSpec(memory_space=pltpu.SMEM)
    got_block = pl.BlockSpec((NX, SENT_ROWS, B), lambda i, where_ref: (0, 0, 0))
    psi_block = pl.BlockSpec((NX, VECS * B, B), lambda i, where_ref: (0, i, 0))
    out_block = pl.BlockSpec((1, NZ, NX * VECS * ROWS, B), lambda i, where_ref: (i, 0, 0, 0))

    def right_y(i, where_ref):
        return (where_ref[1] if mine else 1 - where_ref[1]) * HALF_Y + i

    def kernel(where_ref, owner_ref, pick_ref, got_ref, *rest):
        if mine:
            rest = (got_ref, *rest)
        part_kernel(mine, where_ref, owner_ref, pick_ref, got_ref, *rest)

    return pl.pallas_call(
        kernel,
        out_shape=(out, out),
        grid_spec=pltpu.PrefetchScalarGridSpec(
            num_scalar_prefetch=1,
            grid=(HALF_Y,),
            in_specs=[smem, smem, got_block]
            + ([] if mine else [psi_block])
            + [
                pl.BlockSpec(
                    (1, TERM_DEV * 2, B, B), lambda i, where_ref: (right_y(i, where_ref), 0, 0, 0)
                )
            ],
            out_specs=(out_block, out_block),
            scratch_shapes=[
                pltpu.SMEM((NX * NY + 1,), jnp.int32),
                pltpu.VMEM((2, NZ, NX * VECS * ROWS, B), jnp.bfloat16),
            ],
        ),
        cost_estimate=pl.CostEstimate(
            flops=2 * NY * NX * VECS * TERM_DEV * B**3, bytes_accessed=6 * 2**20, transcendentals=0
        ),
        name="part_own" if mine else "part_other",
    )(where, right_owner, right_pick, got, *(() if mine else (psi,)), right)


def add_kernel(keep_a, taken_a, keep_b, taken_b, out_ref):
    out_ref[0] = (keep_a[...].astype(jnp.float32) + taken_a[...].astype(jnp.float32)).astype(jnp.bfloat16)
    out_ref[1] = (keep_b[...].astype(jnp.float32) + taken_b[...].astype(jnp.float32)).astype(jnp.bfloat16)


def add_rows(keep_a, taken_a, keep_b, taken_b):
    block = (1,) + keep_a.shape[1:]
    return pl.pallas_call(
        add_kernel,
        out_shape=jax.ShapeDtypeStruct((2,) + keep_a.shape, jnp.bfloat16),
        grid=(HALF_Y,),
        in_specs=[pl.BlockSpec(block, lambda i: (i, 0, 0, 0))] * 4,
        out_specs=pl.BlockSpec((2,) + block, lambda i: (0, i, 0, 0, 0)),
        name="add_rows",
    )(keep_a, taken_a, keep_b, taken_b)


def sum_kernel(where_ref, valid_ref, arrived_ref, out_ref):
    first = ((pl.program_id(0) + where_ref[1]) & 1) * HALF_Y * NX
    for y in range(HALF_Y):
        total = arrived_ref[y, 0].astype(jnp.float32)
        for z in range(1, NZ):
            total = total + arrived_ref[y, z].astype(jnp.float32)
        for v in range(VECS):
            blocks = []
            for x in range(NX):
                block = total[(x * VECS + v) * ROWS : (x * VECS + v + 1) * ROWS]
                blocks.append(jnp.where(valid_ref[first + y * NX + x] > 0, block, 0.0))
            out_ref[v, pl.ds(y * NX * ROWS, NX * ROWS)] = jnp.concatenate(blocks, axis=0).astype(jnp.bfloat16)


def sum_rows(where, valid, arrived):
    return pl.pallas_call(
        sum_kernel,
        out_shape=jax.ShapeDtypeStruct((VECS, NY * NX * ROWS, B), jnp.bfloat16),
        grid_spec=pltpu.PrefetchScalarGridSpec(
            num_scalar_prefetch=1,
            grid=(2,),
            in_specs=[
                pl.BlockSpec(memory_space=pltpu.SMEM),
                pl.BlockSpec((HALF_Y,) + arrived.shape[1:], lambda i, where_ref: (i, 0, 0, 0)),
            ],
            out_specs=pl.BlockSpec(
                (VECS, HALF_Y * NX * ROWS, B), lambda i, where_ref: (0, (i + where_ref[1]) & 1, 0)
            ),
        ),
        name="sum_rows",
    )(where, valid, arrived)


def shards(psi, left_env, right_env, left_pick, right_owner, right_pick):
    here = lax.axis_index("sec")
    where = jnp.stack([here, lax.axis_index("term") % 2]).astype(jnp.int32)
    rights = lax.all_gather(
        right_env.reshape(TERM_DEV * 2, B, B), "sec", axis=0, tiled=False, axis_index_groups=Y_GROUPS
    )
    valid = jnp.any(right_owner.reshape(-1, PAIR_DEV) == here, axis=1).astype(jnp.int32)
    sent = pack(where, right_owner, left_pick, psi, left_env.reshape(ENV_ROWS, B))
    got = lax.all_to_all(sent, "sec", 0, 0, tiled=True, axis_index_groups=X_GROUPS)
    other = lax.ppermute(got[:, :PSI_ROWS], "term", CORE_SWAP)
    part = (where, right_owner, right_pick, got)
    keep_own, give_own = part_products(True, *part, None, rights)
    taken_other = lax.ppermute(give_own, "term", CORE_SWAP)
    other, keep_own = lax.optimization_barrier((other, keep_own))
    keep_other, give_other = part_products(False, *part, other, rights)
    taken_own = lax.ppermute(give_other, "term", CORE_SWAP)
    both = add_rows(keep_own, taken_own, keep_other, taken_other)
    both = both.reshape(NY * NZ, NX * VECS * ROWS, B)
    both, valid = lax.optimization_barrier((both, valid))
    arrived = lax.all_to_all(both, ("sec", "term"), 0, 0, tiled=True, axis_index_groups=YZ_GROUPS)
    total = sum_rows(where, valid, arrived.reshape(NY, NZ, NX * VECS * ROWS, B))
    return total.reshape(VECS, NY * NX, ROWS, B)


def solution(mesh):
    return jax.shard_map(
        shards,
        mesh=mesh,
        in_specs=(
            P(None, "sec", None, None),
            P("term", "sec", None, None),
            P("term", "sec", None, None),
            P("sec"),
            P(),
            P(),
        ),
        out_specs=P(None, "sec", "term", None),
        check_vma=False,
    )
```

time: 149 us -> 151 us (1.013)
  the two profiles are of different devices: /device:TPU:16 before, /device:TPU:59 now
where the time goes in v3:
time: 151 us; the launch traced here: 150 us
  blocking collectives  89.3 us (59%)
  Pallas kernels  28.8 us (19%)
  between operations  13.5 us (9%)
  starting transfers between devices  11.3 us (7%)
  local copies, waits for them, and re-layouts  3.65 us (2%)
  waiting for transfers between devices  2.14 us (1%)
    all_to_all x1, blocking collectives, shards(): lax.all_to_all(both, ('sec', 'term'), 0, 0, tiled=True, axis_index_groups...  54.4 us
    all_to_all x1, blocking collectives, shards(): lax.all_to_all(sent, 'sec', 0, 0, tiled=True, axis_index_groups=X_GROUPS)  34.9 us
    pallas_call x2, Pallas kernels, part_products(): pl.pallas_call(kernel, out_shape=(out, out), grid_spec=pltpu.PrefetchScal...  16.7 us
    ppermute x1, starting transfers between devices, shards(): taken_own = lax.ppermute(give_other, 'term', CORE_SWAP)  6.06 us
    pallas_call x1, Pallas kernels, pack(): pl.pallas_call(pack_kernel, out_shape=jax.ShapeDtypeStruct((NX, SENT_ROWS...  5.14 us
    pallas_call x1, Pallas kernels, add_rows(): pl.pallas_call(add_kernel, out_shape=jax.ShapeDtypeStruct((2,) + keep_a.s...  4.05 us
    unnamed x12, local copies, waits for them, and re-layouts  3.47 us
    ppermute x1, starting transfers between devices, shards(): other = lax.ppermute(got[:, :PSI_ROWS], 'term', CORE_SWAP)  3.3 us
  transfers between devices with their start and end apart: 4, of which 1 were waited for; matrix products, arithmetic and copies ran while one was open for 1% of the time, Pallas kernels for 9%

profile of v3, /device:TPU:59, one launch (start us, length us, event | category | flops | bytes accessed | tf_op | source)
XLA Modules:
  0.0 150.0 jit_solution(13728961598791220908)
XLA Ops:
  6.5 0.0 all-gather.2.cloned.1.call-start
  6.5 0.7 all-gather.2.cloned.1.call-update
  7.3 0.6 pad_add_fusion.where_ref
  7.9 5.1 %pack.1 = bf16[4,2576,128]{2,1,0:T(8,128)(2,1)} custom-call(s32[2]{0:T(128)} %pad_add_fusion.where_ref, s32[512]{0:T(512)} %owner_ref.5, s32[16]{0:T(128)} %pick_ref.3, bf16[3,16,128,128]{3,2,1,0:T(8,128)(2,1)} %psi_ref.1, bf16[1024,128]{1,0:T(8,128)(2,1)} %bitcast.9), custom_call_target="tpu_custom_call" | custom-call | tf_op jit(solution)/shard_map/pack/pallas_call | solution.py:78
  13.0 34.9 %all_to_all.10.got_ref = bf16[4,2576,128]{2,1,0:T(8,128)(2,1)S(1)} all-to-all(bf16[4,2576,128]{2,1,0:T(8,128)(2,1)} %pack.1), channel_id=1, replica_groups={{0,16,32,48},{64,80,96,112},{128,144,160,176},{192,208,224,240},{256,27..., dimensions={0} | all-to-all | bytes 5275648 | tf_op jit(solution)/shard_map/all_to_all | solution.py:245
  47.9 0.0 copy-start
  47.9 0.1 slice.4
  48.0 1.4 copy-done
  49.4 3.3 %collective-permute-start = (bf16[4,1536,128]{2,1,0:T(8,128)(2,1)S(1)}, bf16[4,1536,128]{2,1,0:T(8,128)(2,1)S(1)}, u32[]{:S(2)}, u32[]{:S(2)}) collective-permute-start(bf16[4,1536,128]{2,1,0:T(8,128)(2,1)S(1)} %slice.4), channel_id=1, source_target_pairs={{0,1},{1,0},{2,3},{3,2},{4,5},{5,4},{6,7},{7,6},{8,9},{9,8},{10,11... | collective-permute-start | bytes 4718600 | tf_op jit(solution)/shard_map/ppermute | solution.py:246
  52.8 0.0 all-gather.2.cloned.1.call-done.rest_0_.rest_1_
  52.8 8.2 %part_own.1 = (bf16[4,8,96,128]{3,2,1,0:T(8,128)(2,1)}, bf16[4,8,96,128]{3,2,1,0:T(8,128)(2,1)}) custom-call(s32[2]{0:T(128)} %pad_add_fusion.where_ref, s32[512]{0:T(512)} %owner_ref.5, s32[512]{0:T(512)} %pick_ref.5, bf16[4,2576,128]{2,1,0:T(8,128)(2,1)} %copy-done, bf16[8,8,128,128]{3,2,1,0:T(8,128)(2,1)} %all-gather.2.cloned.1.call-done.rest_0_.rest_1_), custom_call_target="tpu_custom_call" | custom-call | flops 1610612736 | bytes 6291456 | tf_op jit(solution)/shard_map/part_own/pallas_call | solution.py:161
  61.0 0.0 collective-permute-done.rest_0_
  61.0 0.0 copy-start.1
  61.0 1.2 copy-done.1
  62.2 0.0 copy-start.5
  62.2 0.0 copy-start.4
  62.2 8.5 %part_other.1 = (bf16[4,8,96,128]{3,2,1,0:T(8,128)(2,1)}, bf16[4,8,96,128]{3,2,1,0:T(8,128)(2,1)}) custom-call(s32[2]{0:T(128)} %pad_add_fusion.where_ref, s32[512]{0:T(512)} %owner_ref.5, s32[512]{0:T(512)} %pick_ref.5, bf16[4,2576,128]{2,1,0:T(8,128)(2,1)} %copy-done, bf16[4,1536,128]{2,1,0:T(8,128)(2,1)} %copy-done.1, ...), custom_call_target="tpu_custom_call" | custom-call | flops 1610612736 | bytes 6291456 | tf_op jit(solution)/shard_map/part_other/pallas_call | solution.py:161
  70.7 6.1 %collective-permute-start.1 = (bf16[4,8,96,128]{3,2,1,0:T(8,128)(2,1)}, bf16[4,8,96,128]{3,2,1,0:T(8,128)(2,1)S(1)}, u32[]{:S(2)}, u32[]{:S(2)}) collective-permute-start(bf16[4,8,96,128]{3,2,1,0:T(8,128)(2,1)} %get-tuple-element.16), channel_id=1, source_target_pairs={{0,1},{1,0},{2,3},{3,2},{4,5},{5,4},{6,7},{7,6},{8,9},{9,8},{10,11... | collective-permute-start | bytes 2359304 | tf_op jit(solution)/shard_map/ppermute | solution.py:252
  76.8 0.0 copy-done.5
  76.8 1.9 %collective-permute-start.2 = (bf16[4,8,96,128]{3,2,1,0:T(8,128)(2,1)S(1)}, bf16[4,8,96,128]{3,2,1,0:T(8,128)(2,1)S(1)}, u32[]{:S(2)}, u32[]{:S(2)}) collective-permute-start(bf16[4,8,96,128]{3,2,1,0:T(8,128)(2,1)S(1)} %copy-done.5), channel_id=1, source_target_pairs={{0,1},{1,0},{2,3},{3,2},{4,5},{5,4},{6,7},{7,6},{8,9},{9,8},{10,11... | collective-permute-start | bytes 2359304 | tf_op jit(solution)/shard_map/ppermute | solution.py:249
  78.7 0.0 copy-done.4
  78.7 0.1 eq.13
  78.8 0.1 reduce_or.9
  78.9 0.6 convert_element_type.3.valid_ref
  79.5 0.0 collective-permute-done.1.taken_a
  79.5 0.0 copy-start.2
  79.6 1.4 collective-permute-done.2.taken_b
  81.0 0.0 copy-start.3
  81.0 0.0 copy-done.2
  81.0 0.9 copy-done.3
  81.8 4.0 %add_rows.1 = bf16[2,4,8,96,128]{4,3,2,1,0:T(8,128)(2,1)} custom-call(bf16[4,8,96,128]{3,2,1,0:T(8,128)(2,1)} %get-tuple-element.14.keep_a, bf16[4,8,96,128]{3,2,1,0:T(8,128)(2,1)} %copy-done.2, bf16[4,8,96,128]{3,2,1,0:T(8,128)(2,1)} %get-tuple-element.17.keep_b, bf16[4,8,96,128]{3,2,1,0:T(8,128)(2,1)} %copy-done.3), custom_call_target="tpu_custom_call" | custom-call | tf_op jit(solution)/shard_map/add_rows/pallas_call | solution.py:194
  85.9 54.4 %all_to_all.11 = bf16[64,96,128]{2,1,0:T(8,128)(2,1)} all-to-all(bf16[64,96,128]{2,1,0:T(8,128)(2,1)} %bitcast.8), channel_id=1, replica_groups={{0,2,4,6,8,10,12,14,64,66,68,70,72,74,76,78,128,130,132,134,136,138,140..., dimensions={0} | all-to-all | bytes 3145728 | tf_op jit(solution)/shard_map/all_to_all | solution.py:256
  140.3 2.8 %sum_rows.1 = bf16[3,256,128]{2,1,0:T(8,128)(2,1)} custom-call(s32[2]{0:T(128)} %pad_add_fusion.where_ref, s32[32]{0:T(128)} %convert_element_type.3.valid_ref, bf16[8,8,96,128]{3,2,1,0:T(8,128)(2,1)} %bitcast.7), custom_call_target="tpu_custom_call" | custom-call | tf_op jit(solution)/shard_map/sum_rows/pallas_call | solution.py:219
  (1 shorter events, 0.0 us)
Async XLA Ops:
  6.5 46.2 %all-gather.2.cloned.1.call-start = ((), (), s32[]{:S(2)}) async-start(), calls=%async_computation.2 | async-start | bytes 2359296 | tf_op jit(solution)/shard_map/all_gather | solution.py:240
  47.9 1.5 %copy-start = (bf16[4,2576,128]{2,1,0:T(8,128)(2,1)}, bf16[4,2576,128]{2,1,0:T(8,128)(2,1)S(1)}, u32[]{:S(2)}) copy-start(bf16[4,2576,128]{2,1,0:T(8,128)(2,1)S(1)} %all_to_all.10.got_ref) | copy-start | bytes 7913476
  49.4 11.6 %collective-permute-start = (bf16[4,1536,128]{2,1,0:T(8,128)(2,1)S(1)}, bf16[4,1536,128]{2,1,0:T(8,128)(2,1)S(1)}, u32[]{:S(2)}, u32[]{:S(2)}) collective-permute-start(bf16[4,1536,128]{2,1,0:T(8,128)(2,1)S(1)} %slice.4), channel_id=1, source_target_pairs={{0,1},{1,0},{2,3},{3,2},{4,5},{5,4},{6,7},{7,6},{8,9},{9,8},{10,11... | collective-permute-start | bytes 4718600 | tf_op jit(solution)/shard_map/ppermute | solution.py:246
  61.0 1.2 copy-start.1
  62.2 14.6 %copy-start.5 = (bf16[4,8,96,128]{3,2,1,0:T(8,128)(2,1)S(1)}, bf16[4,8,96,128]{3,2,1,0:T(8,128)(2,1)}, u32[]{:S(2)}) copy-start(bf16[4,8,96,128]{3,2,1,0:T(8,128)(2,1)} %get-tuple-element.18) | copy-start | bytes 2359300
  62.2 16.5 %copy-start.4 = (s32[512]{0:T(512)S(1)}, s32[512]{0:T(512)}, u32[]{:S(2)}) copy-start(s32[512]{0:T(512)} %owner_ref.5) | copy-start | bytes 6148
  70.7 8.8 %collective-permute-start.1 = (bf16[4,8,96,128]{3,2,1,0:T(8,128)(2,1)}, bf16[4,8,96,128]{3,2,1,0:T(8,128)(2,1)S(1)}, u32[]{:S(2)}, u32[]{:S(2)}) collective-permute-start(bf16[4,8,96,128]{3,2,1,0:T(8,128)(2,1)} %get-tuple-element.16), channel_id=1, source_target_pairs={{0,1},{1,0},{2,3},{3,2},{4,5},{5,4},{6,7},{7,6},{8,9},{9,8},{10,11... | collective-permute-start | bytes 2359304 | tf_op jit(solution)/shard_map/ppermute | solution.py:252
  76.8 4.2 %collective-permute-start.2 = (bf16[4,8,96,128]{3,2,1,0:T(8,128)(2,1)S(1)}, bf16[4,8,96,128]{3,2,1,0:T(8,128)(2,1)S(1)}, u32[]{:S(2)}, u32[]{:S(2)}) collective-permute-start(bf16[4,8,96,128]{3,2,1,0:T(8,128)(2,1)S(1)} %copy-done.5), channel_id=1, source_target_pairs={{0,1},{1,0},{2,3},{3,2},{4,5},{5,4},{6,7},{7,6},{8,9},{9,8},{10,11... | collective-permute-start | bytes 2359304 | tf_op jit(solution)/shard_map/ppermute | solution.py:249
  79.5 1.4 copy-start.2
  81.0 0.9 copy-start.3
Sparse Core Ops, SparseCore 0:
  9.4 42.8 all-gather.1

commit v4 on v0

v4 whole, which is shorter than its diff:
```python
import jax
import jax.numpy as jnp
from jax import lax
from jax.experimental import pallas as pl
from jax.experimental.pallas import tpu as pltpu
from jax.sharding import PartitionSpec as P

B = 128
VECS = 3
PAIR_DEV = 16
TERM_DEV = 4
NX = 4
NY = 8
NZ = 8
HALF_Y = NY // 2
ROWS = 8
CORE_ROWS = B // 2
ENVS = TERM_DEV * 2
PSI_ROWS = HALF_Y * VECS * B
ENV_ROWS = ENVS * CORE_ROWS
PICK_ROWS = 16
SWAP_ROWS = PSI_ROWS + ENV_ROWS
SENT_ROWS = SWAP_ROWS + ENV_ROWS + PICK_ROWS
OUT_ROWS = NX * VECS * ROWS

X_GROUPS = [[y * NX + x for x in range(NX)] for y in range(NY)]
YC_GROUPS = [
    [(y * NX + x) * 2 * NZ + z * 2 + c for y in range(NY) for c in range(2)]
    for x in range(NX)
    for z in range(NZ)
]
YZ_GROUPS = [
    [(y * NX + x) * 2 * NZ + z * 2 + c for y in range(NY) for z in range(NZ)]
    for x in range(NX)
    for c in range(2)
]
CORE_SWAP = [(z * 2 + c, z * 2 + 1 - c) for z in range(NZ) for c in range(2)]


def core_rows(block, c):
    wide = block.astype(jnp.float32)
    parts = [wide[(z * 2 + c) * ROWS : (z * 2 + c + 1) * ROWS] for z in range(NZ)]
    return jnp.concatenate(parts, axis=0).astype(jnp.bfloat16)


def pack_kernel(
    psi_ref,
    left_hbm,
    owner_hbm,
    lpick_hbm,
    rpick_hbm,
    out_ref,
    slot_ref,
    left,
    owner,
    lpick,
    rpick,
    table,
    sems,
    load_sems,
):
    here = lax.axis_index("sec")
    core = lax.axis_index("term") & 1
    loads = [
        pltpu.make_async_copy(owner_hbm, owner, load_sems.at[0]),
        pltpu.make_async_copy(left_hbm, left, load_sems.at[1]),
        pltpu.make_async_copy(lpick_hbm, lpick, load_sems.at[2]),
        pltpu.make_async_copy(rpick_hbm, rpick, load_sems.at[3]),
    ]
    for load in loads:
        load.start()
    for k in range(NX * NY):
        table[k] = 0
        slot_ref[k] = -1
    loads[0].wait()

    def fill(j, _):
        table[owner[here * PAIR_DEV + j]] = j
        return 0

    lax.fori_loop(0, PAIR_DEV, fill, 0, unroll=True)
    copies = []
    for x in range(NX):
        for i in range(HALF_Y):
            src = table[(core * HALF_Y + i) * NX + x]
            for v in range(VECS):
                copies.append(
                    pltpu.make_async_copy(
                        psi_ref.at[v, src],
                        out_ref.at[x, pl.ds((i * VECS + v) * B, B)],
                        sems.at[len(copies)],
                    )
                )
    for copy in copies:
        copy.start()
    loads[1].wait()
    for k in range(ENVS):
        block = left[k]
        for c in range(2):
            part = core_rows(block, c)
            at = pl.multiple_of(PSI_ROWS + (1 - (core ^ c)) * ENV_ROWS + k * CORE_ROWS, CORE_ROWS)
            for x in range(NX):
                out_ref[x, pl.ds(at, CORE_ROWS)] = part
    for load in loads[2:]:
        load.wait()
    row = lax.broadcasted_iota(jnp.int32, (PICK_ROWS, B), 0)
    for x in range(NX):
        value = jnp.zeros((PICK_ROWS, B), jnp.int32)
        for y in range(NY):
            value = jnp.where(row == y, lpick[table[y * NX + x]], value)
        out_ref[x, pl.ds(SENT_ROWS - PICK_ROWS, PICK_ROWS)] = value.astype(jnp.float32).astype(jnp.bfloat16)
    my_x = here & (NX - 1)
    first = (here - my_x) * PAIR_DEV

    def slots(j, _):
        right = owner[first + j]
        slot = lax.shift_right_logical(j, 4) * NY + lax.shift_right_logical(right, 2)
        slot_ref[jnp.where((right & (NX - 1)) == my_x, slot, NX * NY)] = rpick[first + j]
        return 0

    lax.fori_loop(0, NX * PAIR_DEV, slots, 0, unroll=8)
    for copy in copies:
        copy.wait()


def pack(psi, left, right_owner, left_pick, right_pick):
    hbm = pl.BlockSpec(memory_space=pltpu.HBM)
    return pl.pallas_call(
        pack_kernel,
        out_shape=(
            jax.ShapeDtypeStruct((NX, SENT_ROWS, B), jnp.bfloat16),
            jax.ShapeDtypeStruct((NX * NY + 1,), jnp.int32),
        ),
        in_specs=[hbm] * 5,
        out_specs=(pl.BlockSpec(memory_space=pltpu.VMEM), pl.BlockSpec(memory_space=pltpu.SMEM)),
        scratch_shapes=[
            pltpu.VMEM(left.shape, jnp.bfloat16),
            pltpu.SMEM(right_owner.shape, jnp.int32),
            pltpu.SMEM(left_pick.shape, jnp.int32),
            pltpu.SMEM(right_pick.shape, jnp.int32),
            pltpu.SMEM((NX * NY,), jnp.int32),
            pltpu.SemaphoreType.DMA((NX * HALF_Y * VECS,)),
            pltpu.SemaphoreType.DMA((4,)),
        ],
        compiler_params=pltpu.CompilerParams(vmem_limit_bytes=16 * 1024 * 1024),
        name="pack",
    )(psi, left, right_owner, left_pick, right_pick)


def part_kernel(slot_ref, got_ref, other_ref, right_hbm, out_ref, right, rows, sems):
    core = lax.axis_index("term") & 1

    def order(step):
        return ((core * HALF_Y) + step) & (NY - 1)

    def load(step):
        return pltpu.make_async_copy(
            right_hbm.at[pl.ds(order(step) * 2, 2)], right.at[pl.ds(step * 2, 2)], sems.at[step]
        )

    for step in range(NY):
        load(step).start()
    row = lax.broadcasted_iota(jnp.int32, (PICK_ROWS, B), 0)

    def work(step, psi_ref):
        right_y = order(step)
        load(step).wait()
        for x in range(NX):
            pick = slot_ref[x * NY + right_y]

            @pl.when(pick >= 0)
            def _():
                picks = got_ref[x, pl.ds(SENT_ROWS - PICK_ROWS, PICK_ROWS), :].astype(jnp.float32)
                second = jnp.max(jnp.where(row == right_y, picks, 0.0), axis=0, keepdims=True) > 0.5
                second = jnp.broadcast_to(second, (CORE_ROWS, B))
                lefts = []
                for ref, at in ((got_ref, SWAP_ROWS), (other_ref, PSI_ROWS)):
                    for t in range(TERM_DEV):
                        first_env = ref[x, pl.ds(at + (t * 2) * CORE_ROWS, CORE_ROWS), :]
                        second_env = ref[x, pl.ds(at + (t * 2 + 1) * CORE_ROWS, CORE_ROWS), :]
                        lefts.append(jnp.where(second, second_env, first_env))
                lefts = jnp.concatenate(lefts, axis=0)
                rights = jnp.concatenate(
                    [right[step * 2 + c, t * 2 + pick] for c in (core, 1 - core) for t in range(TERM_DEV)],
                    axis=0,
                )
                at = pl.multiple_of((step & (HALF_Y - 1)) * VECS * B, B)
                halves = []
                for v in range(VECS):
                    vec = psi_ref[x, pl.ds(at + v * B, B), :]
                    half = jnp.dot(lefts, vec, preferred_element_type=jnp.float32).astype(jnp.bfloat16)
                    halves.append(
                        jnp.concatenate(
                            [half[t * CORE_ROWS : (t + 1) * CORE_ROWS] for t in range(2 * TERM_DEV)], axis=1
                        )
                    )
                prod = jnp.dot(jnp.concatenate(halves, axis=0), rights, preferred_element_type=jnp.float32)
                for v in range(VECS):
                    for z in range(NZ):
                        rows[z, pl.ds((x * VECS + v) * ROWS, ROWS)] = prod[
                            v * CORE_ROWS + z * ROWS : v * CORE_ROWS + (z + 1) * ROWS
                        ]

        for z in range(NZ):
            out_ref[right_y, z] = rows[z].astype(jnp.bfloat16)

    rows[...] = jnp.zeros_like(rows)
    pl.loop(0, HALF_Y)(lambda step: work(step, got_ref))
    pl.loop(HALF_Y, NY)(lambda step: work(step, other_ref))


def part_products(slots, got, other, right):
    vmem = pl.BlockSpec(memory_space=pltpu.VMEM)
    return pl.pallas_call(
        part_kernel,
        out_shape=jax.ShapeDtypeStruct((NY, NZ, OUT_ROWS, B), jnp.bfloat16),
        in_specs=[
            pl.BlockSpec(memory_space=pltpu.SMEM),
            vmem,
            vmem,
            pl.BlockSpec(memory_space=pltpu.HBM),
        ],
        out_specs=vmem,
        scratch_shapes=[
            pltpu.VMEM((2 * NY, ENVS, B, B), jnp.bfloat16),
            pltpu.VMEM((NZ, OUT_ROWS, B), jnp.float32),
            pltpu.SemaphoreType.DMA((NY,)),
        ],
        compiler_params=pltpu.CompilerParams(vmem_limit_bytes=20 * 1024 * 1024),
        cost_estimate=pl.CostEstimate(
            flops=4 * NY * NX * VECS * TERM_DEV * B**3, bytes_accessed=10 * 2**20, transcendentals=0
        ),
        name="part",
    )(slots, got, other, right)


def shards(psi, left_env, right_env, left_pick, right_owner, right_pick):
    here = lax.axis_index("sec")
    rights = lax.all_gather(
        right_env.reshape(ENVS, B, B), ("sec", "term"), axis=0, tiled=False, axis_index_groups=YC_GROUPS
    )
    valid = jnp.any(right_owner.reshape(-1, PAIR_DEV) == here, axis=1)
    held = (psi, left_env.reshape(ENVS, B, B), right_owner, left_pick, right_pick)
    sent, slots = pack(*(pltpu.with_memory_space_constraint(a, pltpu.HBM) for a in held))
    got = lax.all_to_all(sent, "sec", 0, 0, tiled=True, axis_index_groups=X_GROUPS)
    other = lax.ppermute(got[:, :SWAP_ROWS], "term", CORE_SWAP)
    rights = pltpu.with_memory_space_constraint(rights, pltpu.HBM)
    both = part_products(slots, got, other, rights).reshape(NY * NZ, OUT_ROWS, B)
    both, valid = lax.optimization_barrier((both, valid))
    arrived = lax.all_to_all(both, ("sec", "term"), 0, 0, tiled=True, axis_index_groups=YZ_GROUPS)
    arrived = arrived.reshape(NY, NZ, NX, VECS, ROWS, B)
    total = jnp.sum(arrived.astype(jnp.float32), axis=1)
    total = total.transpose(2, 0, 1, 3, 4).reshape(VECS, NY * NX, ROWS, B)
    return jnp.where(valid[None, :, None, None], total, 0.0).astype(jnp.bfloat16)


def solution(mesh):
    return jax.shard_map(
        shards,
        mesh=mesh,
        in_specs=(
            P(None, "sec", None, None),
            P("term", "sec", None, None),
            P("term", "sec", None, None),
            P("sec"),
            P(),
            P(),
        ),
        out_specs=P(None, "sec", "term", None),
        check_vma=False,
    )
```

time: 461 us -> 132 us (0.29)
  the two profiles are of different devices: /device:TPU:2 before, /device:TPU:18 now
where the time goes in v4:
time: 132 us; the launch traced here: 131 us
  blocking collectives  90.2 us (68%)
  Pallas kernels  14 us (11%)
  between operations  13.4 us (10%)
  waiting for transfers between devices  8.89 us (7%)
  starting transfers between devices  1.91 us (1%)
  local copies, waits for them, and re-layouts  1.57 us (1%)
    all_to_all x1, blocking collectives, shards(): lax.all_to_all(both, ('sec', 'term'), 0, 0, tiled=True, axis_index_groups...  54.9 us
    all_to_all x1, blocking collectives, shards(): lax.all_to_all(sent, 'sec', 0, 0, tiled=True, axis_index_groups=X_GROUPS)  35.3 us
    pallas_call x1, Pallas kernels, part_products(): pl.pallas_call(part_kernel, out_shape=jax.ShapeDtypeStruct((NY, NZ, OUT_R...  10.7 us
    ppermute x1, waiting for transfers between devices, shards(): other = lax.ppermute(got[:, :SWAP_ROWS], 'term', CORE_SWAP)  4.23 us
    all_gather x1, waiting for transfers between devices, shards(): lax.all_gather(right_env.reshape(ENVS, B, B), ('sec', 'term'), axis=0, ti...  3.94 us
    pallas_call x1, Pallas kernels, pack(): pl.pallas_call(pack_kernel, out_shape=(jax.ShapeDtypeStruct((NX, SENT_ROW...  3.3 us
  transfers between devices with their start and end apart: 2, of which 2 were waited for; matrix products, arithmetic and copies ran while one was open for 1% of the time, Pallas kernels for 3%

profile of v4, /device:TPU:18, one launch (start us, length us, event | category | flops | bytes accessed | tf_op | source)
XLA Modules:
  0.0 131.1 jit_solution(7205991228226309463)
XLA Ops:
  6.5 0.0 all-gather.2.cloned.1.call-start
  6.5 0.7 all-gather.2.cloned.1.call-update
  7.3 3.3 %pack.1 = (bf16[4,2576,128]{2,1,0:T(8,128)(2,1)S(1)}, s32[33]{0:T(128)S(1)}) custom-call(bf16[3,16,128,128]{3,2,1,0:T(8,128)(2,1)} %psi_ref.1, bf16[8,128,128]{2,1,0:T(8,128)(2,1)} %bitcast.13, s32[512]{0:T(512)} %owner_hbm.1, s32[16]{0:T(128)} %lpick_hbm.1, s32[512]{0:T(512)} %rpick_hbm.1), custom_call_target="tpu_custom_call" | custom-call | tf_op jit(solution)/shard_map/pack/pallas_call | solution.py:128
  10.6 35.3 %all_to_all.10.got_ref = bf16[4,2576,128]{2,1,0:T(8,128)(2,1)S(1)} all-to-all(bf16[4,2576,128]{2,1,0:T(8,128)(2,1)S(1)} %get-tuple-element.10), channel_id=1, replica_groups={{0,16,32,48},{64,80,96,112},{128,144,160,176},{192,208,224,240},{256,27..., dimensions={0} | all-to-all | bytes 5275648 | tf_op jit(solution)/shard_map/all_to_all | solution.py:245
  45.8 0.0 copy-start
  45.8 1.5 %slice.4 = bf16[4,2048,128]{2,1,0:T(8,128)(2,1)} slice(bf16[4,2576,128]{2,1,0:T(8,128)(2,1)S(1)} %all_to_all.10.got_ref), slice={[0:4], [0:2048], [0:128]} | slice | bytes 4194304 | tf_op jit(solution)/shard_map/slice | solution.py:246
  47.3 1.9 %collective-permute-start = (bf16[4,2048,128]{2,1,0:T(8,128)(2,1)}, bf16[4,2048,128]{2,1,0:T(8,128)(2,1)}, u32[]{:S(2)}, u32[]{:S(2)}) collective-permute-start(bf16[4,2048,128]{2,1,0:T(8,128)(2,1)} %slice.4), channel_id=1, source_target_pairs={{0,1},{1,0},{2,3},{3,2},{4,5},{5,4},{6,7},{7,6},{8,9},{9,8},{10,11... | collective-permute-start | bytes 6291464 | tf_op jit(solution)/shard_map/ppermute | solution.py:246
  49.2 0.0 copy-done
  49.2 0.1 eq.11
  49.3 0.1 reduce_or.9
  49.5 4.2 %collective-permute-done.other_ref = bf16[4,2048,128]{2,1,0:T(8,128)(2,1)} collective-permute-done((bf16[4,2048,128]{2,1,0:T(8,128)(2,1)}, bf16[4,2048,128]{2,1,0:T(8,128)(2,1)}, u32[]{:S(2)}, u32[]{:S(2)}) %collective-permute-start) | collective-permute-done | bytes 2097184 | tf_op jit(solution)/shard_map/ppermute | solution.py:246
  53.7 3.9 %all-gather.2.cloned.1.call-done.right_hbm = bf16[16,8,128,128]{3,2,1,0:T(8,128)(2,1)} async-done(((bf16[1,8,128,128]{3,2,1,0:T(8,128)(2,1)}), bf16[16,8,128,128]{3,2,1,0:T(8,128)(2,1)}) %all-gather.2.cloned.1.call-update) | async-done | bytes 4194320 | tf_op jit(solution)/shard_map/all_gather | solution.py:239
  57.6 10.7 %part.1 = bf16[8,8,96,128]{3,2,1,0:T(8,128)(2,1)S(1)} custom-call(s32[33]{0:T(128)S(1)} %get-tuple-element.9.slot_ref, bf16[4,2576,128]{2,1,0:T(8,128)(2,1)S(1)} %all_to_all.10.got_ref, bf16[4,2048,128]{2,1,0:T(8,128)(2,1)} %collective-permute-done.other_ref, bf16[16,8,128,128]{3,2,1,0:T(8,128)(2,1)} %all-gather.2.cloned.1.call-done.right_hbm), custom_call_target="tpu_custom_call" | custom-call | flops 3221225472 | bytes 10485760 | tf_op jit(solution)/shard_map/part/pallas_call | solution.py:214
  68.3 54.9 %all_to_all.11 = bf16[64,96,128]{2,1,0:T(8,128)(2,1)S(1)} all-to-all(bf16[64,96,128]{2,1,0:T(8,128)(2,1)S(1)} %bitcast.10), channel_id=1, replica_groups={{0,2,4,6,8,10,12,14,64,66,68,70,72,74,76,78,128,130,132,134,136,138,140..., dimensions={0} | all-to-all | bytes 3145728 | tf_op jit(solution)/shard_map/all_to_all | solution.py:250
  123.3 0.2 convert_reduce_fusion
  123.5 0.8 fusion
  (1 shorter events, 0.0 us)
Async XLA Ops:
  6.5 51.1 %all-gather.2.cloned.1.call-start = ((), (), s32[]{:S(2)}) async-start(), calls=%async_computation.2 | async-start | bytes 4456448 | tf_op jit(solution)/shard_map/all_gather | solution.py:239
  45.8 3.4 %copy-start = (s32[512]{0:T(512)S(1)}, s32[512]{0:T(512)}, u32[]{:S(2)}) copy-start(s32[512]{0:T(512)} %owner_hbm.1) | copy-start | bytes 6148
  47.3 6.4 %collective-permute-start = (bf16[4,2048,128]{2,1,0:T(8,128)(2,1)}, bf16[4,2048,128]{2,1,0:T(8,128)(2,1)}, u32[]{:S(2)}, u32[]{:S(2)}) collective-permute-start(bf16[4,2048,128]{2,1,0:T(8,128)(2,1)} %slice.4), channel_id=1, source_target_pairs={{0,1},{1,0},{2,3},{3,2},{4,5},{5,4},{6,7},{7,6},{8,9},{9,8},{10,11... | collective-permute-start | bytes 6291464 | tf_op jit(solution)/shard_map/ppermute | solution.py:246
Sparse Core Ops, SparseCore 0:
  9.5 48.1 all-gather.1

commit v5 on v4

--- a/solution.py
+++ b/solution.py
@@ -22,6 +22,7 @@
 SWAP_ROWS = PSI_ROWS + ENV_ROWS
 SENT_ROWS = SWAP_ROWS + ENV_ROWS + PICK_ROWS
 OUT_ROWS = NX * VECS * ROWS
+LIST = NX * HALF_Y + 2
 
 X_GROUPS = [[y * NX + x for x in range(NX)] for y in range(NY)]
 YC_GROUPS = [
@@ -56,6 +57,7 @@
     lpick,
     rpick,
     table,
+    picks,
     sems,
     load_sems,
 ):
@@ -71,7 +73,7 @@
         load.start()
     for k in range(NX * NY):
         table[k] = 0
-        slot_ref[k] = -1
+        picks[k] = -1
     loads[0].wait()
 
     def fill(j, _):
@@ -115,10 +117,23 @@
     def slots(j, _):
         right = owner[first + j]
         slot = lax.shift_right_logical(j, 4) * NY + lax.shift_right_logical(right, 2)
-        slot_ref[jnp.where((right & (NX - 1)) == my_x, slot, NX * NY)] = rpick[first + j]
+        picks[jnp.where((right & (NX - 1)) == my_x, slot, NX * NY)] = rpick[first + j]
         return 0
 
     lax.fori_loop(0, NX * PAIR_DEV, slots, 0, unroll=8)
+    for side in range(2):
+        base = side * LIST
+
+        def entry(k, count):
+            y = (((core + side) & 1) * HALF_Y) + lax.shift_right_logical(k, 2)
+            x = k & (NX - 1)
+            pick = picks[x * NY + y]
+            slot_ref[base + 1 + count] = (k * 2 + pick) & (2 * NX * HALF_Y - 1)
+            return count + jnp.where(pick >= 0, 1, 0)
+
+        count = lax.fori_loop(0, NX * HALF_Y, entry, 0, unroll=4)
+        slot_ref[base] = lax.shift_right_logical(count + 1, 1)
+        slot_ref[base + 1 + count] = slot_ref[base + jnp.maximum(count, 1)]
     for copy in copies:
         copy.wait()
 
@@ -129,7 +144,7 @@
         pack_kernel,
         out_shape=(
             jax.ShapeDtypeStruct((NX, SENT_ROWS, B), jnp.bfloat16),
-            jax.ShapeDtypeStruct((NX * NY + 1,), jnp.int32),
+            jax.ShapeDtypeStruct((2 * LIST,), jnp.int32),
         ),
         in_specs=[hbm] * 5,
         out_specs=(pl.BlockSpec(memory_space=pltpu.VMEM), pl.BlockSpec(memory_space=pltpu.SMEM)),
@@ -139,6 +154,7 @@
             pltpu.SMEM(left_pick.shape, jnp.int32),
             pltpu.SMEM(right_pick.shape, jnp.int32),
             pltpu.SMEM((NX * NY,), jnp.int32),
+            pltpu.SMEM((NX * NY + 1,), jnp.int32),
             pltpu.SemaphoreType.DMA((NX * HALF_Y * VECS,)),
             pltpu.SemaphoreType.DMA((4,)),
         ],
@@ -150,63 +166,69 @@
 def part_kernel(slot_ref, got_ref, other_ref, right_hbm, out_ref, right, rows, sems):
     core = lax.axis_index("term") & 1
 
-    def order(step):
-        return ((core * HALF_Y) + step) & (NY - 1)
-
-    def load(step):
+    def load(side):
         return pltpu.make_async_copy(
-            right_hbm.at[pl.ds(order(step) * 2, 2)], right.at[pl.ds(step * 2, 2)], sems.at[step]
+            right_hbm.at[pl.ds(((core + side) & 1) * 2 * HALF_Y, 2 * HALF_Y)],
+            right.at[pl.ds(side * 2 * HALF_Y, 2 * HALF_Y)],
+            sems.at[side],
         )
 
-    for step in range(NY):
-        load(step).start()
+    load(0).start()
+    load(1).start()
+    rows[...] = jnp.zeros_like(rows)
     row = lax.broadcasted_iota(jnp.int32, (PICK_ROWS, B), 0)
 
-    def work(step, psi_ref):
-        right_y = order(step)
-        load(step).wait()
-        for x in range(NX):
-            pick = slot_ref[x * NY + right_y]
-
-            @pl.when(pick >= 0)
-            def _():
-                picks = got_ref[x, pl.ds(SENT_ROWS - PICK_ROWS, PICK_ROWS), :].astype(jnp.float32)
-                second = jnp.max(jnp.where(row == right_y, picks, 0.0), axis=0, keepdims=True) > 0.5
-                second = jnp.broadcast_to(second, (CORE_ROWS, B))
-                lefts = []
-                for ref, at in ((got_ref, SWAP_ROWS), (other_ref, PSI_ROWS)):
-                    for t in range(TERM_DEV):
-                        first_env = ref[x, pl.ds(at + (t * 2) * CORE_ROWS, CORE_ROWS), :]
-                        second_env = ref[x, pl.ds(at + (t * 2 + 1) * CORE_ROWS, CORE_ROWS), :]
-                        lefts.append(jnp.where(second, second_env, first_env))
-                lefts = jnp.concatenate(lefts, axis=0)
-                rights = jnp.concatenate(
-                    [right[step * 2 + c, t * 2 + pick] for c in (core, 1 - core) for t in range(TERM_DEV)],
-                    axis=0,
+    def product(side, entry):
+        psi_ref = (got_ref, other_ref)[side]
+        pick, x, i = entry & 1, lax.shift_right_logical(entry, 1) & (NX - 1), lax.shift_right_logical(entry, 3)
+        right_y = ((core + side) & 1) * HALF_Y + i
+        picks = got_ref[x, pl.ds(SENT_ROWS - PICK_ROWS, PICK_ROWS), :].astype(jnp.float32)
+        second = jnp.max(jnp.where(row == right_y, picks, 0.0), axis=0, keepdims=True) > 0.5
+        second = jnp.broadcast_to(second, (CORE_ROWS, B))
+        lefts = []
+        for ref, at in ((got_ref, SWAP_ROWS), (other_ref, PSI_ROWS)):
+            for t in range(TERM_DEV):
+                first_env = ref[x, pl.ds(at + (t * 2) * CORE_ROWS, CORE_ROWS), :]
+                second_env = ref[x, pl.ds(at + (t * 2 + 1) * CORE_ROWS, CORE_ROWS), :]
+                lefts.append(jnp.where(second, second_env, first_env))
+        lefts = jnp.concatenate(lefts, axis=0)
+        at = (side * HALF_Y + i) * 2
+        rights = jnp.concatenate(
+            [right[at + c, t * 2 + pick] for c in (core, 1 - core) for t in range(TERM_DEV)], axis=0
+        )
+        halves = []
+        for v in range(VECS):
+            vec = psi_ref[x, pl.ds(pl.multiple_of((i * VECS + v) * B, B), B), :]
+            half = jnp.dot(lefts, vec, preferred_element_type=jnp.float32).astype(jnp.bfloat16)
+            halves.append(
+                jnp.concatenate(
+                    [half[t * CORE_ROWS : (t + 1) * CORE_ROWS] for t in range(2 * TERM_DEV)], axis=1
                 )
-                at = pl.multiple_of((step & (HALF_Y - 1)) * VECS * B, B)
-                halves = []
-                for v in range(VECS):
-                    vec = psi_ref[x, pl.ds(at + v * B, B), :]
-                    half = jnp.dot(lefts, vec, preferred_element_type=jnp.float32).astype(jnp.bfloat16)
-                    halves.append(
-                        jnp.concatenate(
-                            [half[t * CORE_ROWS : (t + 1) * CORE_ROWS] for t in range(2 * TERM_DEV)], axis=1
-                        )
-                    )
-                prod = jnp.dot(jnp.concatenate(halves, axis=0), rights, preferred_element_type=jnp.float32)
-                for v in range(VECS):
-                    for z in range(NZ):
-                        rows[z, pl.ds((x * VECS + v) * ROWS, ROWS)] = prod[
-                            v * CORE_ROWS + z * ROWS : v * CORE_ROWS + (z + 1) * ROWS
-                        ]
-
+            )
+        prod = jnp.dot(jnp.concatenate(halves, axis=0), rights, preferred_element_type=jnp.float32)
+        return right_y, x, prod
+
+    def store(right_y, x, prod):
+        for v in range(VECS):
+            for z in range(NZ):
+                at = pl.multiple_of((x * VECS + v) * ROWS, ROWS)
+                rows[right_y, z, pl.ds(at, ROWS)] = prod[
+                    v * CORE_ROWS + z * ROWS : v * CORE_ROWS + (z + 1) * ROWS
+                ]
+
+    for side in range(2):
+        load(side).wait()
+
+        def pair(k, _):
+            done = [product(side, slot_ref[side * LIST + 1 + 2 * k + n]) for n in range(2)]
+            for result in done:
+                store(*result)
+            return 0
+
+        lax.fori_loop(0, slot_ref[side * LIST], pair, 0)
+    for y in range(NY):
         for z in range(NZ):
-            out_ref[right_y, z] = rows[z].astype(jnp.bfloat16)
-
-    rows[...] = jnp.zeros_like(rows)
-    pl.loop(0, HALF_Y)(lambda step: work(step, got_ref))
-    pl.loop(HALF_Y, NY)(lambda step: work(step, other_ref))
+            out_ref[y, z] = rows[y, z].astype(jnp.bfloat16)
 
 
 def part_products(slots, got, other, right):
@@ -223,8 +245,8 @@
         out_specs=vmem,
         scratch_shapes=[
             pltpu.VMEM((2 * NY, ENVS, B, B), jnp.bfloat16),
-            pltpu.VMEM((NZ, OUT_ROWS, B), jnp.float32),
-            pltpu.SemaphoreType.DMA((NY,)),
+            pltpu.VMEM((NY, NZ, OUT_ROWS, B), jnp.float32),
+            pltpu.SemaphoreType.DMA((2,)),
         ],
         compiler_params=pltpu.CompilerParams(vmem_limit_bytes=20 * 1024 * 1024),
         cost_estimate=pl.CostEstimate(

time: 132 us -> 130 us (0.985)
  the two profiles are of different devices: /device:TPU:18 before, /device:TPU:16 now
where the time goes in v5:
time: 130 us
  blocking collectives  91 us (70%)
  between operations  13.4 us (10%)
  Pallas kernels  13.1 us (10%)
  waiting for transfers between devices  7.87 us (6%)
  starting transfers between devices  1.91 us (1%)
  local copies, waits for them, and re-layouts  1.57 us (1%)
    all_to_all x1, blocking collectives, shards(): lax.all_to_all(both, ('sec', 'term'), 0, 0, tiled=True, axis_index_groups...  54.8 us
    all_to_all x1, blocking collectives, shards(): lax.all_to_all(sent, 'sec', 0, 0, tiled=True, axis_index_groups=X_GROUPS)  36.3 us
    pallas_call x1, Pallas kernels, part_products(): pl.pallas_call(part_kernel, out_shape=jax.ShapeDtypeStruct((NY, NZ, OUT_R...  9.79 us
    ppermute x1, waiting for transfers between devices, shards(): other = lax.ppermute(got[:, :SWAP_ROWS], 'term', CORE_SWAP)  4.52 us
    pallas_call x1, Pallas kernels, pack(): pl.pallas_call(pack_kernel, out_shape=(jax.ShapeDtypeStruct((NX, SENT_ROW...  3.31 us
    all_gather x1, waiting for transfers between devices, shards(): lax.all_gather(right_env.reshape(ENVS, B, B), ('sec', 'term'), axis=0, ti...  2.65 us
  transfers between devices with their start and end apart: 2, of which 2 were waited for; matrix products, arithmetic and copies ran while one was open for 1% of the time, Pallas kernels for 3%

profile of v5, /device:TPU:16, one launch (start us, length us, event | category | flops | bytes accessed | tf_op | source)
XLA Modules:
  0.0 130.1 jit_solution(5770259905883760983)
XLA Ops:
  6.5 0.0 all-gather.2.cloned.1.call-start
  6.5 0.7 all-gather.2.cloned.1.call-update
  7.3 3.3 %pack.1 = (bf16[4,2576,128]{2,1,0:T(8,128)(2,1)S(1)}, s32[36]{0:T(128)S(1)}) custom-call(bf16[3,16,128,128]{3,2,1,0:T(8,128)(2,1)} %psi_ref.1, bf16[8,128,128]{2,1,0:T(8,128)(2,1)} %bitcast.13, s32[512]{0:T(512)} %owner_hbm.1, s32[16]{0:T(128)} %lpick_hbm.1, s32[512]{0:T(512)} %rpick_hbm.1), custom_call_target="tpu_custom_call" | custom-call | tf_op jit(solution)/shard_map/pack/pallas_call | solution.py:143
  10.6 36.3 %all_to_all.10.got_ref = bf16[4,2576,128]{2,1,0:T(8,128)(2,1)S(1)} all-to-all(bf16[4,2576,128]{2,1,0:T(8,128)(2,1)S(1)} %get-tuple-element.10), channel_id=1, replica_groups={{0,16,32,48},{64,80,96,112},{128,144,160,176},{192,208,224,240},{256,27..., dimensions={0} | all-to-all | bytes 5275648 | tf_op jit(solution)/shard_map/all_to_all | solution.py:267
  46.9 0.0 copy-start
  46.9 1.5 %slice.4 = bf16[4,2048,128]{2,1,0:T(8,128)(2,1)} slice(bf16[4,2576,128]{2,1,0:T(8,128)(2,1)S(1)} %all_to_all.10.got_ref), slice={[0:4], [0:2048], [0:128]} | slice | bytes 4194304 | tf_op jit(solution)/shard_map/slice | solution.py:268
  48.3 1.9 %collective-permute-start = (bf16[4,2048,128]{2,1,0:T(8,128)(2,1)}, bf16[4,2048,128]{2,1,0:T(8,128)(2,1)}, u32[]{:S(2)}, u32[]{:S(2)}) collective-permute-start(bf16[4,2048,128]{2,1,0:T(8,128)(2,1)} %slice.4), channel_id=1, source_target_pairs={{0,1},{1,0},{2,3},{3,2},{4,5},{5,4},{6,7},{7,6},{8,9},{9,8},{10,11... | collective-permute-start | bytes 6291464 | tf_op jit(solution)/shard_map/ppermute | solution.py:268
  50.3 0.0 copy-done
  50.3 0.1 eq.11
  50.4 0.1 reduce_or.9
  50.5 4.5 %collective-permute-done.other_ref = bf16[4,2048,128]{2,1,0:T(8,128)(2,1)} collective-permute-done((bf16[4,2048,128]{2,1,0:T(8,128)(2,1)}, bf16[4,2048,128]{2,1,0:T(8,128)(2,1)}, u32[]{:S(2)}, u32[]{:S(2)}) %collective-permute-start) | collective-permute-done | bytes 2097184 | tf_op jit(solution)/shard_map/ppermute | solution.py:268
  55.0 2.6 %all-gather.2.cloned.1.call-done.right_hbm = bf16[16,8,128,128]{3,2,1,0:T(8,128)(2,1)} async-done(((bf16[1,8,128,128]{3,2,1,0:T(8,128)(2,1)}), bf16[16,8,128,128]{3,2,1,0:T(8,128)(2,1)}) %all-gather.2.cloned.1.call-update) | async-done | bytes 4194320 | tf_op jit(solution)/shard_map/all_gather | solution.py:261
  57.6 9.8 %part.1 = bf16[8,8,96,128]{3,2,1,0:T(8,128)(2,1)S(1)} custom-call(s32[36]{0:T(128)S(1)} %get-tuple-element.9.slot_ref, bf16[4,2576,128]{2,1,0:T(8,128)(2,1)S(1)} %all_to_all.10.got_ref, bf16[4,2048,128]{2,1,0:T(8,128)(2,1)} %collective-permute-done.other_ref, bf16[16,8,128,128]{3,2,1,0:T(8,128)(2,1)} %all-gather.2.cloned.1.call-done.right_hbm), custom_call_target="tpu_custom_call" | custom-call | flops 3221225472 | bytes 10485760 | tf_op jit(solution)/shard_map/part/pallas_call | solution.py:236
  67.4 54.8 %all_to_all.11 = bf16[64,96,128]{2,1,0:T(8,128)(2,1)S(1)} all-to-all(bf16[64,96,128]{2,1,0:T(8,128)(2,1)S(1)} %bitcast.10), channel_id=1, replica_groups={{0,2,4,6,8,10,12,14,64,66,68,70,72,74,76,78,128,130,132,134,136,138,140..., dimensions={0} | all-to-all | bytes 3145728 | tf_op jit(solution)/shard_map/all_to_all | solution.py:272
  122.2 0.2 convert_reduce_fusion
  122.4 0.8 fusion
  (1 shorter events, 0.0 us)
Async XLA Ops:
  6.5 51.1 %all-gather.2.cloned.1.call-start = ((), (), s32[]{:S(2)}) async-start(), calls=%async_computation.2 | async-start | bytes 4456448 | tf_op jit(solution)/shard_map/all_gather | solution.py:261
  46.9 3.4 %copy-start = (s32[512]{0:T(512)S(1)}, s32[512]{0:T(512)}, u32[]{:S(2)}) copy-start(s32[512]{0:T(512)} %owner_hbm.1) | copy-start | bytes 6148
  48.3 6.7 %collective-permute-start = (bf16[4,2048,128]{2,1,0:T(8,128)(2,1)}, bf16[4,2048,128]{2,1,0:T(8,128)(2,1)}, u32[]{:S(2)}, u32[]{:S(2)}) collective-permute-start(bf16[4,2048,128]{2,1,0:T(8,128)(2,1)} %slice.4), channel_id=1, source_target_pairs={{0,1},{1,0},{2,3},{3,2},{4,5},{5,4},{6,7},{7,6},{8,9},{9,8},{10,11... | collective-permute-start | bytes 6291464 | tf_op jit(solution)/shard_map/ppermute | solution.py:268
Sparse Core Ops, SparseCore 0:
  9.5 48.1 all-gather.1

commit v6 on v5

--- a/solution.py
+++ b/solution.py
@@ -166,15 +166,16 @@
 def part_kernel(slot_ref, got_ref, other_ref, right_hbm, out_ref, right, rows, sems):
     core = lax.axis_index("term") & 1
 
-    def load(side):
+    def load(side, i):
         return pltpu.make_async_copy(
-            right_hbm.at[pl.ds(((core + side) & 1) * 2 * HALF_Y, 2 * HALF_Y)],
-            right.at[pl.ds(side * 2 * HALF_Y, 2 * HALF_Y)],
-            sems.at[side],
+            right_hbm.at[pl.ds((((core + side) & 1) * HALF_Y + i) * 2, 2)],
+            right.at[pl.ds((side * HALF_Y + i) * 2, 2)],
+            sems.at[side * HALF_Y + i],
         )
 
-    load(0).start()
-    load(1).start()
+    for side in range(2):
+        for i in range(HALF_Y):
+            load(side, i).start()
     rows[...] = jnp.zeros_like(rows)
     row = lax.broadcasted_iota(jnp.int32, (PICK_ROWS, B), 0)
 
@@ -217,15 +218,29 @@
                 ]
 
     for side in range(2):
-        load(side).wait()
-
-        def pair(k, _):
-            done = [product(side, slot_ref[side * LIST + 1 + 2 * k + n]) for n in range(2)]
+        first = side * LIST + 1
+        pairs = slot_ref[side * LIST]
+
+        def arrive(seen, upto):
+            def wait(i, _):
+                load(side, i).wait()
+                return 0
+
+            lax.fori_loop(seen, upto, wait, 0)
+            return jnp.maximum(seen, upto)
+
+        def some(count, start, seen):
+            entries = [slot_ref[first + start + n] for n in range(count)]
+            seen = arrive(seen, lax.shift_right_logical(entries[-1], 3) + 1)
+            done = [product(side, entry) for entry in entries]
             for result in done:
                 store(*result)
-            return 0
-
-        lax.fori_loop(0, slot_ref[side * LIST], pair, 0)
+            return seen
+
+        fours = lax.shift_right_logical(pairs, 1)
+        seen = lax.fori_loop(0, fours, lambda k, seen: some(4, 4 * k, seen), jnp.int32(0))
+        seen = lax.fori_loop(0, pairs & 1, lambda k, seen: some(2, 4 * fours, seen), seen)
+        arrive(seen, HALF_Y)
     for y in range(NY):
         for z in range(NZ):
             out_ref[y, z] = rows[y, z].astype(jnp.bfloat16)
@@ -246,7 +261,7 @@
         scratch_shapes=[
             pltpu.VMEM((2 * NY, ENVS, B, B), jnp.bfloat16),
             pltpu.VMEM((NY, NZ, OUT_ROWS, B), jnp.float32),
-            pltpu.SemaphoreType.DMA((2,)),
+            pltpu.SemaphoreType.DMA((NY,)),
         ],
         compiler_params=pltpu.CompilerParams(vmem_limit_bytes=20 * 1024 * 1024),
         cost_estimate=pl.CostEstimate(
@@ -265,7 +280,7 @@
     held = (psi, left_env.reshape(ENVS, B, B), right_owner, left_pick, right_pick)
     sent, slots = pack(*(pltpu.with_memory_space_constraint(a, pltpu.HBM) for a in held))
     got = lax.all_to_all(sent, "sec", 0, 0, tiled=True, axis_index_groups=X_GROUPS)
-    other = lax.ppermute(got[:, :SWAP_ROWS], "term", CORE_SWAP)
+    other = lax.ppermute(got, "term", CORE_SWAP)
     rights = pltpu.with_memory_space_constraint(rights, pltpu.HBM)
     both = part_products(slots, got, other, rights).reshape(NY * NZ, OUT_ROWS, B)
     both, valid = lax.optimization_barrier((both, valid))

time: 130 us -> 130 us (level)
  Pallas kernels: 13.1 us -> 11.4 us
  waiting for transfers between devices: 7.87 us -> 9.41 us
  local copies, waits for them, and re-layouts: 1.57 us -> 0.09 us
    pallas_call x1, Pallas kernels: 9.79 us -> 8.14 us  [part_products(): pl.pallas_call(part_kernel, out_shape=jax.ShapeDtypeStruct((NY, NZ, OUT_R...]
    slice x1 -> x0, local copies, waits for them, and re-layouts: 1.47 us -> none  [shards(): other = lax.ppermute(got[:, :SWAP_ROWS], 'term', CORE_SWAP)]
  transfers between devices with their start and end apart: 2 -> 2, of which waited for: 2 -> 2; matrix products, arithmetic and copies ran while one was open for 1% -> 0% of each run, Pallas kernels for 3% -> 3%
where the time goes in v6:
time: 130 us
  blocking collectives  92.3 us (71%)
  between operations  13.4 us (10%)
  Pallas kernels  11.4 us (9%)
  waiting for transfers between devices  9.41 us (7%)
  starting transfers between devices  1.91 us (1%)
    all_to_all x1, blocking collectives, shards(): lax.all_to_all(both, ('sec', 'term'), 0, 0, tiled=True, axis_index_groups...  56 us
    all_to_all x1, blocking collectives, shards(): lax.all_to_all(sent, 'sec', 0, 0, tiled=True, axis_index_groups=X_GROUPS)  36.3 us
    pallas_call x1, Pallas kernels, part_products(): pl.pallas_call(part_kernel, out_shape=jax.ShapeDtypeStruct((NY, NZ, OUT_R...  8.14 us
    ppermute x1, waiting for transfers between devices, shards(): other = lax.ppermute(got, 'term', CORE_SWAP)  4.8 us
    all_gather x1, waiting for transfers between devices, shards(): lax.all_gather(right_env.reshape(ENVS, B, B), ('sec', 'term'), axis=0, ti...  3.91 us
    pallas_call x1, Pallas kernels, pack(): pl.pallas_call(pack_kernel, out_shape=(jax.ShapeDtypeStruct((NX, SENT_ROW...  3.27 us
  transfers between devices with their start and end apart: 2, of which 2 were waited for; matrix products, arithmetic and copies ran while one was open for 0% of the time, Pallas kernels for 3%

profile of v6, /device:TPU:16, one launch (start us, length us, event | category | flops | bytes accessed | tf_op | source)
XLA Modules:
  0.0 129.7 jit_solution(16887043562606227349)
XLA Ops:
  6.5 0.0 all-gather.2.cloned.1.call-start
  6.5 0.7 all-gather.2.cloned.1.call-update
  7.3 3.3 %pack.1 = (bf16[4,2576,128]{2,1,0:T(8,128)(2,1)S(1)}, s32[36]{0:T(128)S(1)}) custom-call(bf16[3,16,128,128]{3,2,1,0:T(8,128)(2,1)} %psi_ref.1, bf16[8,128,128]{2,1,0:T(8,128)(2,1)} %bitcast.13, s32[512]{0:T(512)} %owner_hbm.1, s32[16]{0:T(128)} %lpick_hbm.1, s32[512]{0:T(512)} %rpick_hbm.1), custom_call_target="tpu_custom_call" | custom-call | tf_op jit(solution)/shard_map/pack/pallas_call | solution.py:143
  10.5 0.0 copy-start
  10.5 36.3 %all_to_all.10.got_ref = bf16[4,2576,128]{2,1,0:T(8,128)(2,1)S(1)} all-to-all(bf16[4,2576,128]{2,1,0:T(8,128)(2,1)S(1)} %get-tuple-element.10), channel_id=1, replica_groups={{0,16,32,48},{64,80,96,112},{128,144,160,176},{192,208,224,240},{256,27..., dimensions={0} | all-to-all | bytes 5275648 | tf_op jit(solution)/shard_map/all_to_all | solution.py:282
  46.8 1.9 %collective-permute-start = (bf16[4,2576,128]{2,1,0:T(8,128)(2,1)S(1)}, bf16[4,2576,128]{2,1,0:T(8,128)(2,1)}, u32[]{:S(2)}, u32[]{:S(2)}) collective-permute-start(bf16[4,2576,128]{2,1,0:T(8,128)(2,1)S(1)} %all_to_all.10.got_ref), channel_id=1, source_target_pairs={{0,1},{1,0},{2,3},{3,2},{4,5},{5,4},{6,7},{7,6},{8,9},{9,8},{10,11... | collective-permute-start | bytes 7913480 | tf_op jit(solution)/shard_map/ppermute | solution.py:283
  48.7 0.0 copy-done
  48.7 0.1 eq.11
  48.8 0.1 reduce_or.9
  48.9 4.8 %collective-permute-done.other_ref = bf16[4,2576,128]{2,1,0:T(8,128)(2,1)} collective-permute-done((bf16[4,2576,128]{2,1,0:T(8,128)(2,1)S(1)}, bf16[4,2576,128]{2,1,0:T(8,128)(2,1)}, u32[]{:S(2)}, u32[]{:S(2)}) %collective-permute-start) | collective-permute-done | bytes 2637856 | tf_op jit(solution)/shard_map/ppermute | solution.py:283
  53.7 3.9 %all-gather.2.cloned.1.call-done.right_hbm = bf16[16,8,128,128]{3,2,1,0:T(8,128)(2,1)} async-done(((bf16[1,8,128,128]{3,2,1,0:T(8,128)(2,1)}), bf16[16,8,128,128]{3,2,1,0:T(8,128)(2,1)}) %all-gather.2.cloned.1.call-update) | async-done | bytes 4194320 | tf_op jit(solution)/shard_map/all_gather | solution.py:276
  57.7 8.1 %part.1 = bf16[8,8,96,128]{3,2,1,0:T(8,128)(2,1)S(1)} custom-call(s32[36]{0:T(128)S(1)} %get-tuple-element.9.slot_ref, bf16[4,2576,128]{2,1,0:T(8,128)(2,1)S(1)} %all_to_all.10.got_ref, bf16[4,2576,128]{2,1,0:T(8,128)(2,1)} %collective-permute-done.other_ref, bf16[16,8,128,128]{3,2,1,0:T(8,128)(2,1)} %all-gather.2.cloned.1.call-done.right_hbm), custom_call_target="tpu_custom_call" | custom-call | flops 3221225472 | bytes 10485760 | tf_op jit(solution)/shard_map/part/pallas_call | solution.py:251
  65.8 56.0 %all_to_all.11 = bf16[64,96,128]{2,1,0:T(8,128)(2,1)S(1)} all-to-all(bf16[64,96,128]{2,1,0:T(8,128)(2,1)S(1)} %bitcast.10), channel_id=1, replica_groups={{0,2,4,6,8,10,12,14,64,66,68,70,72,74,76,78,128,130,132,134,136,138,140..., dimensions={0} | all-to-all | bytes 3145728 | tf_op jit(solution)/shard_map/all_to_all | solution.py:287
  121.8 0.2 convert_reduce_fusion
  122.1 0.8 fusion
  (1 shorter events, 0.0 us)
Async XLA Ops:
  6.5 51.1 %all-gather.2.cloned.1.call-start = ((), (), s32[]{:S(2)}) async-start(), calls=%async_computation.2 | async-start | bytes 4456448 | tf_op jit(solution)/shard_map/all_gather | solution.py:276
  10.5 38.2 %copy-start = (s32[512]{0:T(512)S(1)}, s32[512]{0:T(512)}, u32[]{:S(2)}) copy-start(s32[512]{0:T(512)} %owner_hbm.1) | copy-start | bytes 6148
  46.8 6.9 %collective-permute-start = (bf16[4,2576,128]{2,1,0:T(8,128)(2,1)S(1)}, bf16[4,2576,128]{2,1,0:T(8,128)(2,1)}, u32[]{:S(2)}, u32[]{:S(2)}) collective-permute-start(bf16[4,2576,128]{2,1,0:T(8,128)(2,1)S(1)} %all_to_all.10.got_ref), channel_id=1, source_target_pairs={{0,1},{1,0},{2,3},{3,2},{4,5},{5,4},{6,7},{7,6},{8,9},{9,8},{10,11... | collective-permute-start | bytes 7913480 | tf_op jit(solution)/shard_map/ppermute | solution.py:283
Sparse Core Ops, SparseCore 0:
  9.5 48.1 all-gather.1

commit v7 on v6

--- a/solution.py
+++ b/solution.py
@@ -120,7 +120,7 @@
         picks[jnp.where((right & (NX - 1)) == my_x, slot, NX * NY)] = rpick[first + j]
         return 0
 
-    lax.fori_loop(0, NX * PAIR_DEV, slots, 0, unroll=8)
+    lax.fori_loop(0, NX * PAIR_DEV, slots, 0, unroll=True)
     for side in range(2):
         base = side * LIST
 
@@ -131,7 +131,7 @@
             slot_ref[base + 1 + count] = (k * 2 + pick) & (2 * NX * HALF_Y - 1)
             return count + jnp.where(pick >= 0, 1, 0)
 
-        count = lax.fori_loop(0, NX * HALF_Y, entry, 0, unroll=4)
+        count = lax.fori_loop(0, NX * HALF_Y, entry, 0, unroll=True)
         slot_ref[base] = lax.shift_right_logical(count + 1, 1)
         slot_ref[base + 1 + count] = slot_ref[base + jnp.maximum(count, 1)]
     for copy in copies:

time: 130 us -> 130 us (level)
  no operation moved by 1% of the time
where the time goes in v7:
time: 130 us; the launch traced here: 129 us
  blocking collectives  91.5 us (70%)
  between operations  13.4 us (10%)
  Pallas kernels  11.8 us (9%)
  waiting for transfers between devices  9.49 us (7%)
  starting transfers between devices  1.91 us (1%)
    all_to_all x1, blocking collectives, shards(): lax.all_to_all(both, ('sec', 'term'), 0, 0, tiled=True, axis_index_groups...  55.4 us
    all_to_all x1, blocking collectives, shards(): lax.all_to_all(sent, 'sec', 0, 0, tiled=True, axis_index_groups=X_GROUPS)  36.2 us
    pallas_call x1, Pallas kernels, part_products(): pl.pallas_call(part_kernel, out_shape=jax.ShapeDtypeStruct((NY, NZ, OUT_R...  8.53 us
    ppermute x1, waiting for transfers between devices, shards(): other = lax.ppermute(got, 'term', CORE_SWAP)  4.8 us
    all_gather x1, waiting for transfers between devices, shards(): lax.all_gather(right_env.reshape(ENVS, B, B), ('sec', 'term'), axis=0, ti...  3.99 us
    pallas_call x1, Pallas kernels, pack(): pl.pallas_call(pack_kernel, out_shape=(jax.ShapeDtypeStruct((NX, SENT_ROW...  3.28 us
  transfers between devices with their start and end apart: 2, of which 2 were waited for; matrix products, arithmetic and copies ran while one was open for 0% of the time, Pallas kernels for 3%

profile of v7, /device:TPU:16, one launch (start us, length us, event | category | flops | bytes accessed | tf_op | source)
XLA Modules:
  0.0 129.4 jit_solution(8142847934432721051)
XLA Ops:
  6.5 0.0 all-gather.2.cloned.1.call-start
  6.5 0.7 all-gather.2.cloned.1.call-update
  7.3 3.3 %pack.1 = (bf16[4,2576,128]{2,1,0:T(8,128)(2,1)S(1)}, s32[36]{0:T(128)S(1)}) custom-call(bf16[3,16,128,128]{3,2,1,0:T(8,128)(2,1)} %psi_ref.1, bf16[8,128,128]{2,1,0:T(8,128)(2,1)} %bitcast.13, s32[512]{0:T(512)} %owner_hbm.1, s32[16]{0:T(128)} %lpick_hbm.1, s32[512]{0:T(512)} %rpick_hbm.1), custom_call_target="tpu_custom_call" | custom-call | tf_op jit(solution)/shard_map/pack/pallas_call | solution.py:143
  10.5 0.0 copy-start
  10.6 36.2 %all_to_all.10.got_ref = bf16[4,2576,128]{2,1,0:T(8,128)(2,1)S(1)} all-to-all(bf16[4,2576,128]{2,1,0:T(8,128)(2,1)S(1)} %get-tuple-element.10), channel_id=1, replica_groups={{0,16,32,48},{64,80,96,112},{128,144,160,176},{192,208,224,240},{256,27..., dimensions={0} | all-to-all | bytes 5275648 | tf_op jit(solution)/shard_map/all_to_all | solution.py:282
  46.7 1.9 %collective-permute-start = (bf16[4,2576,128]{2,1,0:T(8,128)(2,1)S(1)}, bf16[4,2576,128]{2,1,0:T(8,128)(2,1)}, u32[]{:S(2)}, u32[]{:S(2)}) collective-permute-start(bf16[4,2576,128]{2,1,0:T(8,128)(2,1)S(1)} %all_to_all.10.got_ref), channel_id=1, source_target_pairs={{0,1},{1,0},{2,3},{3,2},{4,5},{5,4},{6,7},{7,6},{8,9},{9,8},{10,11... | collective-permute-start | bytes 7913480 | tf_op jit(solution)/shard_map/ppermute | solution.py:283
  48.6 0.0 copy-done
  48.7 0.1 eq.11
  48.8 0.1 reduce_or.9
  48.9 4.8 %collective-permute-done.other_ref = bf16[4,2576,128]{2,1,0:T(8,128)(2,1)} collective-permute-done((bf16[4,2576,128]{2,1,0:T(8,128)(2,1)S(1)}, bf16[4,2576,128]{2,1,0:T(8,128)(2,1)}, u32[]{:S(2)}, u32[]{:S(2)}) %collective-permute-start) | collective-permute-done | bytes 2637856 | tf_op jit(solution)/shard_map/ppermute | solution.py:283
  53.7 4.0 %all-gather.2.cloned.1.call-done.right_hbm = bf16[16,8,128,128]{3,2,1,0:T(8,128)(2,1)} async-done(((bf16[1,8,128,128]{3,2,1,0:T(8,128)(2,1)}), bf16[16,8,128,128]{3,2,1,0:T(8,128)(2,1)}) %all-gather.2.cloned.1.call-update) | async-done | bytes 4194320 | tf_op jit(solution)/shard_map/all_gather | solution.py:276
  57.7 8.5 %part.1 = bf16[8,8,96,128]{3,2,1,0:T(8,128)(2,1)S(1)} custom-call(s32[36]{0:T(128)S(1)} %get-tuple-element.9.slot_ref, bf16[4,2576,128]{2,1,0:T(8,128)(2,1)S(1)} %all_to_all.10.got_ref, bf16[4,2576,128]{2,1,0:T(8,128)(2,1)} %collective-permute-done.other_ref, bf16[16,8,128,128]{3,2,1,0:T(8,128)(2,1)} %all-gather.2.cloned.1.call-done.right_hbm), custom_call_target="tpu_custom_call" | custom-call | flops 3221225472 | bytes 10485760 | tf_op jit(solution)/shard_map/part/pallas_call | solution.py:251
  66.2 55.4 %all_to_all.11 = bf16[64,96,128]{2,1,0:T(8,128)(2,1)S(1)} all-to-all(bf16[64,96,128]{2,1,0:T(8,128)(2,1)S(1)} %bitcast.10), channel_id=1, replica_groups={{0,2,4,6,8,10,12,14,64,66,68,70,72,74,76,78,128,130,132,134,136,138,140..., dimensions={0} | all-to-all | bytes 3145728 | tf_op jit(solution)/shard_map/all_to_all | solution.py:287
  121.5 0.2 convert_reduce_fusion
  121.8 0.8 fusion
  (1 shorter events, 0.0 us)
Async XLA Ops:
  6.5 51.1 %all-gather.2.cloned.1.call-start = ((), (), s32[]{:S(2)}) async-start(), calls=%async_computation.2 | async-start | bytes 4456448 | tf_op jit(solution)/shard_map/all_gather | solution.py:276
  10.5 38.1 %copy-start = (s32[512]{0:T(512)S(1)}, s32[512]{0:T(512)}, u32[]{:S(2)}) copy-start(s32[512]{0:T(512)} %owner_hbm.1) | copy-start | bytes 6148
  46.7 6.9 %collective-permute-start = (bf16[4,2576,128]{2,1,0:T(8,128)(2,1)S(1)}, bf16[4,2576,128]{2,1,0:T(8,128)(2,1)}, u32[]{:S(2)}, u32[]{:S(2)}) collective-permute-start(bf16[4,2576,128]{2,1,0:T(8,128)(2,1)S(1)} %all_to_all.10.got_ref), channel_id=1, source_target_pairs={{0,1},{1,0},{2,3},{3,2},{4,5},{5,4},{6,7},{7,6},{8,9},{9,8},{10,11... | collective-permute-start | bytes 7913480 | tf_op jit(solution)/shard_map/ppermute | solution.py:283
Sparse Core Ops, SparseCore 0:
  9.5 48.1 all-gather.1
